TPU v7x, 256 devices: a whole 4x4x8 slice. The times are simulated.
256 devices in a mesh: gx: 8 (over z_hi, core), gy: 4 (over y), gz: 8 (over z_lo, x).
Axes of the slice: x: 4, y: 4, z: 8 (z_hi: 4, z_lo: 2; z = z_hi * 2 + z_lo), core: 2. Of those that a mesh axis runs over, the one named last changes fastest.
Arguments:
- volume: bfloat16 [4, 32, 128, 512], P(None, 'gx', 'gz', 'gy'), may hold values from -6 to 6
- first_filters: float32 [32, 108], replicated, may hold values from -0.625 to 0.625
- first_bias: float32 [32], replicated, may hold values from -3 to 3
- second_filters: float32 [64, 864], replicated, may hold values from -0.21875 to 0.21875
- second_bias: float32 [64], replicated, may hold values from -3 to 3
- cotangent: bfloat16 [64, 8, 32, 128], P(None, 'gx', 'gz', 'gy'), may hold values from -6 to 6
Outputs:
- features: bfloat16 [64, 8, 32, 128], P(None, 'gx', 'gz', 'gy')
- stepped_first: float32 [32, 108], replicated
- offset_first: float32 [32], replicated
- stepped_second: float32 [64, 864], replicated
- offset_second: float32 [64], replicated
All inputs are finite; a program needn't handle non-finite values.
Results may differ from a plain program's by a relative error of at most 0.0015.
The roundings to bfloat16 on the way count: a program that leaves them out, or rounds other values in their place, can miss the bound.
Values may be sent and summed in bfloat16 or wider, within the bound.
A program may use at most 128 MiB of HBM per device.

v0:
```python
import jax
import jax.numpy as jnp
from jax import lax
from jax.sharding import PartitionSpec as P

negative_slope = 0.3
learn_rate = 0.001


def extended(cells, sides, width):
    for axis, dim in sides:
        count = lax.axis_size(axis)
        ends = count - 1
        head = lax.slice_in_dim(cells, 0, width, axis=dim)
        tail = lax.slice_in_dim(cells, cells.shape[dim] - width, cells.shape[dim], axis=dim)
        cells = jnp.concatenate(
            [
                lax.ppermute(tail, axis, [(i, (i + 1) % count) for i in range(ends)]),
                cells,
                lax.ppermute(head, axis, [((i + 1) % count, i) for i in range(ends)]),
            ],
            axis=dim,
        )
    return cells


def leaky_relu(tensor):
    return jnp.where(tensor > 0, tensor, negative_slope * tensor)


def slopes(tensor):
    return jnp.where(tensor > 0, 1.0, negative_slope).astype(tensor.dtype)


def pool_pairs(tensor):
    channels, wide_cells, deep_cells, high_cells = tensor.shape
    blocks = tensor.reshape(channels, wide_cells // 2, 2, deep_cells // 2, 2, high_cells // 2, 2)
    return jnp.mean(blocks, axis=(2, 4, 6))


def spread(tensor):
    channels, wide_cells, deep_cells, high_cells = tensor.shape
    expanded = jnp.broadcast_to(
        tensor[:, :, None, :, None, :, None],
        (channels, wide_cells, 2, deep_cells, 2, high_cells, 2),
    )
    return expanded.reshape(channels, 2 * wide_cells, 2 * deep_cells, 2 * high_cells)


def columns(padded, wide_cells, deep_cells, high_cells, flipped):
    pieces = []
    for i in range(3):
        for j in range(3):
            for k in range(3):
                if flipped:
                    start_w, start_d, start_h = (2 - i, 2 - j, 2 - k)
                else:
                    start_w, start_d, start_h = (i, j, k)
                pieces.append(
                    padded[
                        :,
                        start_w : start_w + wide_cells,
                        start_d : start_d + deep_cells,
                        start_h : start_h + high_cells,
                    ]
                )
    return jnp.stack(pieces, 0).reshape(-1, wide_cells * deep_cells * high_cells)


def contract_cells(errors, gathered):
    return lax.dot_general(
        errors, gathered, (((1,), (1,)), ((), ())), preferred_element_type=jnp.float32
    )


def shards(volume, first_filters, first_bias, second_filters, second_bias, cotangent):
    channels, wide_cells, deep_cells, high_cells = volume.shape
    half_w, half_d, half_h = (wide_cells // 2, deep_cells // 2, high_cells // 2)
    padded = extended(volume, (("gx", 1), ("gz", 2), ("gy", 3)), 1)
    volume_cols = columns(padded, wide_cells, deep_cells, high_cells, False)
    first_half = first_filters.astype(jnp.bfloat16)
    second_half = second_filters.astype(jnp.bfloat16)
    mid_channels = first_filters.shape[0]
    out_channels = second_filters.shape[0]
    first_pre = (
        jnp.dot(first_half, volume_cols, preferred_element_type=jnp.float32) + first_bias[:, None]
    ).reshape(mid_channels, wide_cells, deep_cells, high_cells)
    pooled = pool_pairs(leaky_relu(first_pre)).astype(jnp.bfloat16)
    pooled_padded = extended(pooled, (("gx", 1), ("gz", 2), ("gy", 3)), 1)
    pooled_cols = columns(pooled_padded, half_w, half_d, half_h, False)
    second_pre = (
        jnp.dot(second_half, pooled_cols, preferred_element_type=jnp.float32) + second_bias[:, None]
    ).reshape(out_channels, half_w, half_d, half_h)
    second_error = (spread(cotangent.astype(jnp.float32)) * 0.125 * slopes(second_pre)).astype(
        jnp.bfloat16
    )
    error_padded = extended(second_error, (("gx", 1), ("gz", 2), ("gy", 3)), 1)
    features = pool_pairs(leaky_relu(second_pre)).astype(jnp.bfloat16)
    error_flat = second_error.reshape(out_channels, -1)
    second_grad = contract_cells(error_flat, pooled_cols)
    second_bias_grad = jnp.sum(error_flat.astype(jnp.float32), axis=1)
    error_cols = columns(error_padded, half_w, half_d, half_h, True)
    transposed = (
        second_half.reshape(out_channels, 27, mid_channels)
        .transpose(2, 1, 0)
        .reshape(mid_channels, 27 * out_channels)
    )
    pooled_error = (
        jnp.dot(transposed, error_cols, preferred_element_type=jnp.float32)
        .reshape(mid_channels, half_w, half_d, half_h)
        .astype(jnp.bfloat16)
    )
    first_error = (spread(pooled_error.astype(jnp.float32)) * 0.125 * slopes(first_pre)).astype(
        jnp.bfloat16
    )
    first_flat = first_error.reshape(mid_channels, -1)
    first_grad = contract_cells(first_flat, volume_cols)
    first_bias_grad = jnp.sum(first_flat.astype(jnp.float32), axis=1)
    first_total, first_bias_total, second_total, second_bias_total = lax.psum(
        (first_grad, first_bias_grad, second_grad, second_bias_grad), ("gx", "gy", "gz")
    )
    stepped_second = second_filters - learn_rate * second_total
    return (
        features,
        first_filters - learn_rate * first_total,
        first_bias - learn_rate * first_bias_total,
        stepped_second,
        second_bias - learn_rate * second_bias_total,
    )


def solution(mesh):
    return jax.shard_map(
        shards,
        mesh=mesh,
        in_specs=(P(None, "gx", "gz", "gy"), P(), P(), P(), P(), P(None, "gx", "gz", "gy")),
        out_specs=(P(None, "gx", "gz", "gy"), P(), P(), P(), P()),
        check_vma=False,
    )
```

profile of v0, /device:TPU:1, one launch (start us, length us, event | category | flops | bytes accessed | tf_op | source)
XLA Modules:
  0.0 422.0 jit_solution(9309497951105441471)
XLA Ops:
  8.0 6.3 %collective-permute-start = (bf16[4,1,16,128]{3,2,1,0:T(8,128)(2,1)S(1)}, bf16[4,1,16,128]{3,2,1,0:T(8,128)(2,1)S(1)}, u32[]{:S(2)}, u32[]{:S(2)}) collective-permute-start(bf16[4,1,16,128]{3,2,1,0:T(8,128)(2,1)S(1)} %get-tuple-element.38), channel_id=1, source_target_pairs={{0,32},{32,64},{64,96},{96,128},{128,160},{160,192},{192,224},{1,3... | collective-permute-start | bytes 49160 | tf_op jit(solution)/shard_map/ppermute | solution.py:18
  17.1 3.2 collective-permute-done.1
  20.3 3.1 collective-permute-start.2
  24.7 3.1 collective-permute-done.3
  28.0 3.2 collective-permute-start.4
  33.9 4.1 collective-permute-done.5
  58.9 2.7 reshape.156
  62.0 2.7 copy.86
  64.6 6.3 %fusion.1 = f32[32,2,8,64]{0,3,2,1:T(8,128)S(1)} fusion(f32[32,2,2,8,2,64,2]{0,6,5,4,3,2,1:T(2,128)} %bitcast.351), kind=kLoop, calls=%fused_computation.3 | loop fusion | flops 1015808 | bytes 1179648 | tf_op jit(solution)/shard_map/reduce_sum | solution.py:38
  71.8 5.1 %collective-permute-start.6 = (bf16[32,1,8,64]{0,3,2,1:T(8,128)(2,1)S(1)}, bf16[32,1,8,64]{0,3,2,1:T(8,128)(2,1)S(1)}, u32[]{:S(2)}, u32[]{:S(2)}) collective-permute-start(bf16[32,1,8,64]{0,3,2,1:T(8,128)(2,1)S(1)} %get-tuple-element.29), channel_id=1, source_target_pairs={{0,32},{32,64},{64,96},{96,128},{128,160},{160,192},{192,224},{1,3... | collective-permute-start | bytes 98312 | tf_op jit(solution)/shard_map/ppermute | solution.py:18
  78.8 6.7 %collective-permute-done.7 = bf16[32,1,8,64]{0,3,2,1:T(8,128)(2,1)S(1)} collective-permute-done((bf16[32,1,8,64]{0,3,2,1:T(8,128)(2,1)S(1)}, bf16[32,1,8,64]{0,3,2,1:T(8,128)(2,1)S(1)}, u32[]{:S(2)}, u32[]{:S(2)}) %collective-permute-start.7) | collective-permute-done | bytes 32800 | tf_op jit(solution)/shard_map/ppermute | solution.py:20
  86.2 3.1 collective-permute-start.8
  103.0 3.2 collective-permute-start.10
  132.4 8.1 %copy.87 = bf16[27,32,2,8,64]{4,3,2,1,0:T(8,128)(2,1)} copy(bf16[27,32,2,8,64]{1,4,3,2,0:T(8,128)(2,1)} %fusion.38) | data formatting | bytes 3538944 | tf_op jit(solution)/shard_map/stack | solution.py:67
  140.5 6.0 %reshape.158 = bf16[864,1024]{1,0:T(8,128)(2,1)} reshape(bf16[27,32,2,8,64]{4,3,2,1,0:T(8,128)(2,1)} %copy.87) | data formatting | bytes 3538944 | tf_op jit(solution)/shard_map/reshape | solution.py:67
  146.5 3.4 convert_reduce_fusion.1
  153.4 3.4 collective-permute-start.12
  158.8 2.8 fusion.87
  163.6 2.3 collective-permute-done.13
  166.1 5.4 %collective-permute-start.14 = (bf16[64,4,1,64]{3,2,1,0:T(2,128)(2,1)S(1)}, bf16[64,4,1,64]{3,2,1,0:T(2,128)(2,1)S(1)}, u32[]{:S(2)}, u32[]{:S(2)}) collective-permute-start(bf16[64,4,1,64]{3,2,1,0:T(2,128)(2,1)S(1)} %get-tuple-element.20), channel_id=1, source_target_pairs={{0,1},{1,2},{2,3},{3,4},{4,5},{5,6},{6,7},{8,9},{9,10},{10,11},{11... | collective-permute-start | bytes 98312 | tf_op jit(solution)/shard_map/ppermute | solution.py:18
  180.5 2.7 copy.91
  184.5 2.7 copy.93
  187.3 4.6 %collective-permute-start.17 = (bf16[64,4,10,1]{0,1,3,2:T(4,128)(2,1)}, bf16[64,4,10,1]{0,1,3,2:T(4,128)(2,1)}, u32[]{:S(2)}, u32[]{:S(2)}) collective-permute-start(bf16[64,4,10,1]{0,1,3,2:T(4,128)(2,1)} %copy.93), channel_id=1, source_target_pairs={{0,8},{8,16},{16,24},{1,9},{9,17},{17,25},{2,10},{10,18},{18,26},{... | collective-permute-start | bytes 15368 | tf_op jit(solution)/shard_map/ppermute | solution.py:18
  195.2 3.3 copy.92
  198.5 3.3 copy.94
  201.8 4.0 maximum_maximum_fusion
  229.2 10.2 %reshape.160 = bf16[1728,1024]{1,0:T(8,128)(2,1)} reshape(bf16[27,64,2,8,64]{4,3,2,1,0:T(8,128)(2,1)} %fusion.8) | data formatting | bytes 7077888 | tf_op jit(solution)/shard_map/reshape | solution.py:67
  239.4 2.8 fusion.5
  242.4 4.0 broadcast_in_dim.36
  246.4 3.7 copy.98
  252.3 79.8 %all-reduce = (f32[32,108]{1,0:T(8,128)S(1)}, f32[32]{0:T(128)S(1)}, f32[64]{0:T(128)S(1)}) all-reduce(f32[32,108]{1,0:T(8,128)S(1)} %fusion.86, f32[32]{0:T(128)S(1)} %get-tuple-element.10, f32[64]{0:T(128)S(1)} %copy-done.10), channel_id=1, replica_groups=mesh['gx'=8,'gy'=4,'gz'=8] {'gx','gy','gz'}, use_global_device_ids=true, to_apply=%region_2.3 | all-reduce | flops 3552 | bytes 28416 | tf_op jit(solution)/shard_map/psum | solution.py:119
  333.7 79.8 %all-reduce.3.cloned.1.call-done = f32[64,864]{1,0:T(8,128)} async-done(((f32[64,864]{1,0:T(8,128)}), f32[64,864]{1,0:T(8,128)}) %all-reduce.3.cloned.1.call-update) | async-done | bytes 221200 | tf_op jit(solution)/shard_map/psum | solution.py:119
  (173 shorter events, 122.6 us)
Async XLA Ops:
  7.2 54.4 %copy-start.9 = (f32[32,108]{1,0:T(8,128)S(1)}, f32[32,108]{1,0:T(8,128)}, u32[]{:S(2)}) copy-start(f32[32,108]{1,0:T(8,128)} %param.7) | copy-start | bytes 41476
  7.2 54.4 %copy-start.11 = (f32[32]{0:T(128)S(1)}, f32[32]{0:T(128)}, u32[]{:S(2)}) copy-start(f32[32]{0:T(128)} %param.8) | copy-start | bytes 388
  7.2 406.3 %all-reduce.3.cloned.1.call-start = ((), (), s32[]{:S(2)}) async-start(), calls=%async_computation | async-start | bytes 458752 | tf_op jit(solution)/shard_map/psum | solution.py:119
  8.0 8.2 %collective-permute-start = (bf16[4,1,16,128]{3,2,1,0:T(8,128)(2,1)S(1)}, bf16[4,1,16,128]{3,2,1,0:T(8,128)(2,1)S(1)}, u32[]{:S(2)}, u32[]{:S(2)}) collective-permute-start(bf16[4,1,16,128]{3,2,1,0:T(8,128)(2,1)S(1)} %get-tuple-element.38), channel_id=1, source_target_pairs={{0,32},{32,64},{64,96},{96,128},{128,160},{160,192},{192,224},{1,3... | collective-permute-start | bytes 49160 | tf_op jit(solution)/shard_map/ppermute | solution.py:18
  14.3 6.0 %collective-permute-start.1 = (bf16[4,1,16,128]{3,2,1,0:T(8,128)(2,1)S(1)}, bf16[4,1,16,128]{3,2,1,0:T(8,128)(2,1)S(1)}, u32[]{:S(2)}, u32[]{:S(2)}) collective-permute-start(bf16[4,1,16,128]{3,2,1,0:T(8,128)(2,1)S(1)} %get-tuple-element.37), channel_id=1, source_target_pairs={{32,0},{64,32},{96,64},{128,96},{160,128},{192,160},{224,192},{33,... | collective-permute-start | bytes 49160 | tf_op jit(solution)/shard_map/ppermute | solution.py:20
  20.3 4.4 %collective-permute-start.2 = (bf16[4,6,1,128]{3,2,1,0:T(2,128)(2,1)S(1)}, bf16[4,6,1,128]{3,2,1,0:T(2,128)(2,1)S(1)}, u32[]{:S(2)}, u32[]{:S(2)}) collective-permute-start(bf16[4,6,1,128]{3,2,1,0:T(2,128)(2,1)S(1)} %get-tuple-element.35), channel_id=1, source_target_pairs={{0,1},{1,2},{2,3},{3,4},{4,5},{5,6},{6,7},{8,9},{9,10},{10,11},{11... | collective-permute-start | bytes 18440 | tf_op jit(solution)/shard_map/ppermute | solution.py:18
  23.4 4.4 %collective-permute-start.3 = (bf16[4,6,1,128]{3,2,1,0:T(2,128)(2,1)S(1)}, bf16[4,6,1,128]{3,2,1,0:T(2,128)(2,1)S(1)}, u32[]{:S(2)}, u32[]{:S(2)}) collective-permute-start(bf16[4,6,1,128]{3,2,1,0:T(2,128)(2,1)S(1)} %get-tuple-element.36), channel_id=1, source_target_pairs={{1,0},{2,1},{3,2},{4,3},{5,4},{6,5},{7,6},{9,8},{10,9},{11,10},{12... | collective-permute-start | bytes 18440 | tf_op jit(solution)/shard_map/ppermute | solution.py:20
  28.0 5.9 %collective-permute-start.4 = (bf16[4,6,18,1]{3,2,1,0:T(8,128)(2,1)S(1)}, bf16[4,6,18,1]{3,2,1,0:T(8,128)(2,1)S(1)}, u32[]{:S(2)}, u32[]{:S(2)}) collective-permute-start(bf16[4,6,18,1]{3,2,1,0:T(8,128)(2,1)S(1)} %get-tuple-element.32), channel_id=1, source_target_pairs={{0,8},{8,16},{16,24},{1,9},{9,17},{17,25},{2,10},{10,18},{18,26},{... | collective-permute-start | bytes 2600 | tf_op jit(solution)/shard_map/ppermute | solution.py:18
  31.2 6.8 %collective-permute-start.5 = (bf16[4,6,18,1]{3,2,1,0:T(8,128)(2,1)S(1)}, bf16[4,6,18,1]{3,2,1,0:T(8,128)(2,1)S(1)}, u32[]{:S(2)}, u32[]{:S(2)}) collective-permute-start(bf16[4,6,18,1]{3,2,1,0:T(8,128)(2,1)S(1)} %get-tuple-element.31), channel_id=1, source_target_pairs={{8,0},{16,8},{24,16},{9,1},{17,9},{25,17},{10,2},{18,10},{26,18},{... | collective-permute-start | bytes 2600 | tf_op jit(solution)/shard_map/ppermute | solution.py:20
  70.9 0.8 copy-start
  71.8 7.0 %collective-permute-start.6 = (bf16[32,1,8,64]{0,3,2,1:T(8,128)(2,1)S(1)}, bf16[32,1,8,64]{0,3,2,1:T(8,128)(2,1)S(1)}, u32[]{:S(2)}, u32[]{:S(2)}) collective-permute-start(bf16[32,1,8,64]{0,3,2,1:T(8,128)(2,1)S(1)} %get-tuple-element.29), channel_id=1, source_target_pairs={{0,32},{32,64},{64,96},{96,128},{128,160},{160,192},{192,224},{1,3... | collective-permute-start | bytes 98312 | tf_op jit(solution)/shard_map/ppermute | solution.py:18
  76.9 8.6 %collective-permute-start.7 = (bf16[32,1,8,64]{0,3,2,1:T(8,128)(2,1)S(1)}, bf16[32,1,8,64]{0,3,2,1:T(8,128)(2,1)S(1)}, u32[]{:S(2)}, u32[]{:S(2)}) collective-permute-start(bf16[32,1,8,64]{0,3,2,1:T(8,128)(2,1)S(1)} %get-tuple-element.30), channel_id=1, source_target_pairs={{32,0},{64,32},{96,64},{128,96},{160,128},{192,160},{224,192},{33,... | collective-permute-start | bytes 98312 | tf_op jit(solution)/shard_map/ppermute | solution.py:20
  86.2 16.0 %collective-permute-start.8 = (bf16[32,4,1,64]{0,3,2,1:T(8,128)(2,1)}, bf16[32,4,1,64]{0,3,2,1:T(8,128)(2,1)S(1)}, u32[]{:S(2)}, u32[]{:S(2)}) collective-permute-start(bf16[32,4,1,64]{0,3,2,1:T(8,128)(2,1)} %get-tuple-element.24), channel_id=1, source_target_pairs={{0,1},{1,2},{2,3},{3,4},{4,5},{5,6},{6,7},{8,9},{9,10},{10,11},{11... | collective-permute-start | bytes 49160 | tf_op jit(solution)/shard_map/ppermute | solution.py:18
  89.3 12.9 %collective-permute-start.9 = (bf16[32,4,1,64]{0,3,2,1:T(8,128)(2,1)}, bf16[32,4,1,64]{0,3,2,1:T(8,128)(2,1)}, u32[]{:S(2)}, u32[]{:S(2)}) collective-permute-start(bf16[32,4,1,64]{0,3,2,1:T(8,128)(2,1)} %get-tuple-element.25), channel_id=1, source_target_pairs={{1,0},{2,1},{3,2},{4,3},{5,4},{6,5},{7,6},{9,8},{10,9},{11,10},{12... | collective-permute-start | bytes 49160 | tf_op jit(solution)/shard_map/ppermute | solution.py:20
  102.2 19.6 %copy-start.1 = (f32[32,2,8,64]{0,3,2,1:T(8,128)S(1)}, f32[32,2,8,64]{0,3,2,1:T(8,128)}, u32[]{:S(2)}) copy-start(f32[32,2,8,64]{0,3,2,1:T(8,128)} %copy-done) | copy-start | bytes 393220
  103.0 5.7 %collective-permute-start.10 = (bf16[32,4,10,1]{0,3,2,1:T(2,128)(2,1)S(1)}, bf16[32,4,10,1]{0,3,2,1:T(2,128)(2,1)S(1)}, u32[]{:S(2)}, u32[]{:S(2)}) collective-permute-start(bf16[32,4,10,1]{0,3,2,1:T(2,128)(2,1)S(1)} %get-tuple-element.19), channel_id=1, source_target_pairs={{0,8},{8,16},{16,24},{1,9},{9,17},{17,25},{2,10},{10,18},{18,26},{... | collective-permute-start | bytes 7688 | tf_op jit(solution)/shard_map/ppermute | solution.py:18
  106.2 4.5 %collective-permute-start.11 = (bf16[32,4,10,1]{0,3,2,1:T(2,128)(2,1)S(1)}, bf16[32,4,10,1]{0,3,2,1:T(2,128)(2,1)S(1)}, u32[]{:S(2)}, u32[]{:S(2)}) collective-permute-start(bf16[32,4,10,1]{0,3,2,1:T(2,128)(2,1)S(1)} %get-tuple-element.18), channel_id=1, source_target_pairs={{8,0},{16,8},{24,16},{9,1},{17,9},{25,17},{10,2},{18,10},{26,18},{... | collective-permute-start | bytes 7688 | tf_op jit(solution)/shard_map/ppermute | solution.py:20
  140.5 11.0 %copy-start.5 = (f32[64,8,64]{2,1,0:T(8,128)S(1)}, f32[64,8,64]{2,1,0:T(8,128)}, u32[]{:S(2)}) copy-start(f32[64,8,64]{2,1,0:T(8,128)} %copy.90) | copy-start | bytes 393220
  149.9 0.7 copy-start.4
  153.4 10.2 %collective-permute-start.12 = (bf16[64,1,8,64]{3,2,1,0:T(8,128)(2,1)}, bf16[64,1,8,64]{3,2,1,0:T(8,128)(2,1)S(1)}, u32[]{:S(2)}, u32[]{:S(2)}) collective-permute-start(bf16[64,1,8,64]{3,2,1,0:T(8,128)(2,1)} %get-tuple-element.27), channel_id=1, source_target_pairs={{0,32},{32,64},{64,96},{96,128},{128,160},{160,192},{192,224},{1,3... | collective-permute-start | bytes 196616 | tf_op jit(solution)/shard_map/ppermute | solution.py:18
  156.9 9.0 %collective-permute-start.13 = (bf16[64,1,8,64]{3,2,1,0:T(8,128)(2,1)}, bf16[64,1,8,64]{3,2,1,0:T(8,128)(2,1)S(1)}, u32[]{:S(2)}, u32[]{:S(2)}) collective-permute-start(bf16[64,1,8,64]{3,2,1,0:T(8,128)(2,1)} %get-tuple-element.28), channel_id=1, source_target_pairs={{32,0},{64,32},{96,64},{128,96},{160,128},{192,160},{224,192},{33,... | collective-permute-start | bytes 196616 | tf_op jit(solution)/shard_map/ppermute | solution.py:20
  166.1 8.9 %collective-permute-start.14 = (bf16[64,4,1,64]{3,2,1,0:T(2,128)(2,1)S(1)}, bf16[64,4,1,64]{3,2,1,0:T(2,128)(2,1)S(1)}, u32[]{:S(2)}, u32[]{:S(2)}) collective-permute-start(bf16[64,4,1,64]{3,2,1,0:T(2,128)(2,1)S(1)} %get-tuple-element.20), channel_id=1, source_target_pairs={{0,1},{1,2},{2,3},{3,4},{4,5},{5,6},{6,7},{8,9},{9,10},{10,11},{11... | collective-permute-start | bytes 98312 | tf_op jit(solution)/shard_map/ppermute | solution.py:18
  171.5 5.7 %collective-permute-start.15 = (bf16[64,4,1,64]{3,2,1,0:T(2,128)(2,1)S(1)}, bf16[64,4,1,64]{3,2,1,0:T(2,128)(2,1)S(1)}, u32[]{:S(2)}, u32[]{:S(2)}) collective-permute-start(bf16[64,4,1,64]{3,2,1,0:T(2,128)(2,1)S(1)} %get-tuple-element.21), channel_id=1, source_target_pairs={{1,0},{2,1},{3,2},{4,3},{5,4},{6,5},{7,6},{9,8},{10,9},{11,10},{12... | collective-permute-start | bytes 98312 | tf_op jit(solution)/shard_map/ppermute | solution.py:20
  183.2 11.9 %collective-permute-start.16 = (bf16[64,4,10,1]{0,1,3,2:T(4,128)(2,1)}, bf16[64,4,10,1]{0,1,3,2:T(4,128)(2,1)}, u32[]{:S(2)}, u32[]{:S(2)}) collective-permute-start(bf16[64,4,10,1]{0,1,3,2:T(4,128)(2,1)} %copy.91), channel_id=1, source_target_pairs={{8,0},{16,8},{24,16},{9,1},{17,9},{25,17},{10,2},{18,10},{26,18},{... | collective-permute-start | bytes 15368 | tf_op jit(solution)/shard_map/ppermute | solution.py:20
  187.3 11.3 %collective-permute-start.17 = (bf16[64,4,10,1]{0,1,3,2:T(4,128)(2,1)}, bf16[64,4,10,1]{0,1,3,2:T(4,128)(2,1)}, u32[]{:S(2)}, u32[]{:S(2)}) collective-permute-start(bf16[64,4,10,1]{0,1,3,2:T(4,128)(2,1)} %copy.93), channel_id=1, source_target_pairs={{0,8},{8,16},{16,24},{1,9},{9,17},{17,25},{2,10},{10,18},{18,26},{... | collective-permute-start | bytes 15368 | tf_op jit(solution)/shard_map/ppermute | solution.py:18
  201.8 13.3 %copy-start.3 = (bf16[64,4,1,64]{3,2,1,0:T(2,128)(2,1)S(1)}, bf16[64,4,1,64]{3,2,1,0:T(2,128)(2,1)}, u32[]{:S(2)}) copy-start(bf16[64,4,1,64]{3,2,1,0:T(2,128)(2,1)} %copy-done.2) | copy-start | bytes 98308
  201.8 15.8 %copy-start.6 = (f32[64,8,64]{2,1,0:T(8,128)S(1)}, f32[64,8,64]{2,1,0:T(8,128)}, u32[]{:S(2)}) copy-start(f32[64,8,64]{2,1,0:T(8,128)} %copy.90) | copy-start | bytes 393220
  201.8 15.8 %copy-start.7 = (f32[1,64,2,8,64]{4,3,2,1,0:T(8,128)S(1)}, f32[1,64,2,8,64]{4,3,2,1,0:T(8,128)}, u32[]{:S(2)}) copy-start(f32[1,64,2,8,64]{4,3,2,1,0:T(8,128)} %select_n.43) | copy-start | bytes 786436
  242.4 9.9 %copy-start.10 = (f32[64]{0:T(128)S(1)}, f32[64]{0:T(128)}, u32[]{:S(2)}) copy-start(f32[64]{0:T(128)} %get-tuple-element.8) | copy-start | bytes 772
  242.4 90.3 %copy-start.13 = (f32[64]{0:T(128)S(1)}, f32[64]{0:T(128)}, u32[]{:S(2)}) copy-start(f32[64]{0:T(128)} %param.10) | copy-start | bytes 772
  242.4 90.8 %copy-start.12 = (f32[32]{0:T(128)S(1)}, f32[32]{0:T(128)}, u32[]{:S(2)}) copy-start(f32[32]{0:T(128)} %param.8) | copy-start | bytes 388
  246.4 167.1 %copy-start.8 = (f32[64,864]{1,0:T(8,128)S(1)}, f32[64,864]{1,0:T(8,128)}, u32[]{:S(2)}) copy-start(f32[64,864]{1,0:T(8,128)} %param.9) | copy-start | bytes 663556
  (1 other events, 0.6 us)
Sparse Core Ops, SparseCore 0:
  161.8 251.7 all-reduce.2
where the time goes:
time: 425 us; the launch traced here: 422 us
  local copies, waits for them, and re-layouts  118 us (28%)
  waiting for transfers between devices  105 us (25%)
  blocking collectives  79.8 us (19%)
  starting transfers between devices  51.1 us (12%)
  other arithmetic  43.3 us (10%)
  between operations  14.4 us (3%)
  matrix products  10.1 us (2%)
    psum x1, waiting for transfers between devices, shards(): lax.psum((first_grad, first_bias_grad, second_grad, second_bias_grad), ('...  79.8 us
    psum x1, blocking collectives, shards(): lax.psum((first_grad, first_bias_grad, second_grad, second_bias_grad), ('...  79.8 us
    unnamed x89, local copies, waits for them, and re-layouts  49.3 us
    ppermute x9, starting transfers between devices, extended(): lax.ppermute(tail, axis, [(i, (i + 1) % count) for i in range(ends)])  37.4 us
    ppermute x9, waiting for transfers between devices, extended(): lax.ppermute(head, axis, [((i + 1) % count, i) for i in range(ends)])  23.6 us
    reshape x3, local copies, waits for them, and re-layouts, columns(): jnp.stack(pieces, 0).reshape(-1, wide_cells * deep_cells * high_cells)  18.8 us
    unnamed x20, other arithmetic  17.4 us
    ppermute x9, starting transfers between devices, extended(): lax.ppermute(head, axis, [((i + 1) % count, i) for i in range(ends)])  13.7 us
  transfers between devices with their start and end apart: 19, of which 9 were waited for; matrix products, arithmetic and copies ran while one was open for 21% of the time, Pallas kernels for 0%

commit v1 on v0

v1 whole, which is shorter than its diff:
```python
import functools

import jax
import jax.numpy as jnp
import numpy as np
from jax import lax
from jax.experimental import pallas as pl
from jax.experimental.pallas import tpu as pltpu
from jax.sharding import PartitionSpec as P

slope_below = 0.3
learn_rate = 0.001
f32 = jnp.float32
bf16 = jnp.bfloat16
MESH = pl.DeviceIdType.MESH
NN = (((1,), (0,)), ((), ()))
NT = (((1,), (1,)), ((), ()))
TN = (((0,), (0,)), ((), ()))


def mm(a, b, dims=NN):
    return lax.dot_general(a, b, dims, preferred_element_type=f32)


def tables():
    edge = np.zeros((32, 256))
    for r in range(16):
        edge[r, r * 16] = 1
        edge[16 + r, r * 16 + 15] = 1
    place = np.zeros((512, 480))
    for wp in range(6):
        for dp in range(18):
            for ch in range(4):
                w, d = wp - 1, dp - 1
                inner_w, inner_d = 0 <= w < 4, 0 <= d < 16
                if inner_w and inner_d:
                    src = (ch * 4 + w) * 16 + d
                elif inner_d:
                    src = 256 + (64 if w > 0 else 0) + ch * 16 + d
                elif inner_w:
                    src = 384 + (16 if d > 0 else 0) + ch * 4 + w
                else:
                    a, b = int(w > 0), int(d > 0)
                    src = 416 + (a * 2 + b) * 16 + ch * 4 + (0 if a else 3)
                place[(wp * 18 + dp) * 4 + ch, src] = 1
    shift1 = np.zeros((128, 384))
    for l in range(128):
        if l:
            shift1[l - 1, l] = 1
        shift1[l, 128 + l] = 1
        if l < 127:
            shift1[l + 1, 256 + l] = 1
    pick1 = np.zeros((16, 128))
    pick1[0, 0] = pick1[1, 127] = 1
    put1 = np.zeros((32, 384))
    put1[1, 0] = 1
    put1[16, 256 + 127] = 1
    shift2 = np.zeros((128, 384))
    swapped = np.zeros((128, 384))
    for l in range(128):
        for k in range(3):
            s = l % 64 + k - 1
            if 0 <= s < 64:
                s += l - l % 64
                shift2[s, k * 128 + l] = 1
                swapped[(s + 64) % 128, k * 128 + l] = 1
    pick2 = np.zeros((16, 128))
    pick2s = np.zeros((16, 128))
    for r, l in enumerate((0, 63, 64, 127)):
        pick2[r, l] = 1
        pick2s[r, (l + 64) % 128] = 1
    put2 = np.zeros((32, 384))
    put2[1, 0] = put2[3, 64] = 1
    put2[16, 256 + 63] = put2[18, 256 + 127] = 1
    even = np.zeros((256, 128))
    for half in range(2):
        for h in range(64):
            even[half * 128 + 2 * h, half * 64 + h] = 1
    twice = np.zeros((128, 256))
    for half in range(2):
        for h in range(128):
            twice[half * 64 + h // 2, half * 128 + h] = 1
    spread = np.zeros((128, 256))
    gather = np.zeros((256, 128))
    for dc in range(4):
        for hc in range(32):
            for t in range(2):
                spread[dc * 32 + hc, (dc % 2) * 128 + (dc // 2) * 64 + 2 * hc + t] = 1
            gather[(dc % 2) * 128 + (dc // 2) * 64 + 2 * hc, dc * 32 + hc] = 1
    widen = np.zeros((108, 144))
    for q in range(108):
        widen[q, (q // 12) * 16 + q % 12] = 1
    ident = np.zeros((64, 256))
    for o in range(64):
        ident[o, o] = ident[o, 128 + 64 + o] = 1
    every = dict(
        edge=edge, place=place, shift1=shift1, pick1=pick1, put1=put1, shift2=shift2, swapped=swapped,
        pick2=pick2, pick2s=pick2s, put2=put2, even=even, twice=twice, spread=spread, gather=gather,
        widen=widen, narrow=widen.T, ident=ident,
    )
    return {name: value.astype(jnp.bfloat16) for name, value in every.items()}


def row_to_column(row):
    n = row.shape[1]
    diagonal = lax.broadcasted_iota(jnp.int32, (n, n), 0) == lax.broadcasted_iota(jnp.int32, (n, n), 1)
    return jnp.sum(jnp.where(diagonal, jnp.broadcast_to(row, (n, n)), 0.0), axis=1, keepdims=True)


def column_to_row(column):
    n = column.shape[0]
    diagonal = lax.broadcasted_iota(jnp.int32, (n, n), 0) == lax.broadcasted_iota(jnp.int32, (n, n), 1)
    return jnp.sum(jnp.where(diagonal, jnp.broadcast_to(column, (n, n)), 0.0), axis=0, keepdims=True)


def kept(flag, value):
    return lax.select(flag, value, jnp.zeros_like(value))


def leaky(a):
    return jnp.where(a > 0, a, slope_below * a)


def slope(a):
    return jnp.where(a > 0, 1.0, slope_below)


def split3(a):
    high = a.astype(bf16)
    rest = a - high.astype(f32)
    mid = rest.astype(bf16)
    return high, mid, (rest - mid.astype(f32)).astype(bf16)


TABLE_NAMES = (
    "edge", "place", "shift1", "pick1", "put1", "shift2", "swapped", "pick2", "pick2s", "put2",
    "even", "twice", "spread", "gather", "widen", "narrow", "ident",
)


def kernel(sizes, *refs):
    GX, GY, GZ, NX = sizes
    ZL = GZ // NX
    ZH = GX // 2
    NZ = ZH * ZL
    vol, filt1, bias1, filt2, bias2, cot = refs[:6]
    t = dict(zip(TABLE_NAMES, refs[6:6 + len(TABLE_NAMES)]))
    refs = refs[6 + len(TABLE_NAMES):]
    feat, step1, off1, step2, off2 = refs[:5]
    (
        edges, wide_in, deep_in, corner_in, col1, col1_in, xs, pre1, summed,
        pooled, wide2, deep2, corner2, v2, col2, col2_in, ys,
        errs, wide3, deep3, corner3, v3, col3, col3_in, fs, turned, perr,
        grads, core_in, red1, x_in, red2, y_in, red3, z_in, total, send_sems, recv_sems,
    ) = refs[5:]

    gx, gy, gz = lax.axis_index("gx"), lax.axis_index("gy"), lax.axis_index("gz")
    core, zh = lax.rem(gx, 2), lax.div(gx, 2)
    xc, zl = lax.rem(gz, NX), lax.div(gz, NX)
    zc = zh * ZL + zl

    def shifted(dx, dy, dz):
        return (lax.rem(gx + (dx + GX), GX), lax.rem(gy + (dy + GY), GY), lax.rem(gz + (dz + GZ), GZ))

    sibling = (gx + 1 - 2 * core, gy, gz)

    def x_peer(r):
        p = lax.rem(xc + r, NX)
        return p, (gx, gy, zl * NX + p)

    def y_peer(r):
        p = lax.rem(gy + r, GY)
        return p, (gx, p, gz)

    def z_peer(r):
        p = lax.rem(zc + r, NZ)
        return (2 * lax.div(p, ZL) + core, gy, lax.rem(p, ZL) * NX + xc)

    ring = [(dx, dz) for dx in (-1, 0, 1) for dz in (-1, 0, 1) if (dx, dz) != (0, 0)]
    peers = [shifted(dx, 0, dz) for dx, dz in ring]
    peers += [shifted(0, -1, 0), shifted(0, 1, 0), sibling]
    peers += [x_peer(r)[1] for r in range(1, NX)]
    peers += [y_peer(r)[1] for r in range(1, GY)]
    peers += [z_peer(r) for r in range(1, NZ)]
    barrier = pltpu.get_barrier_semaphore()
    for peer in peers:
        pl.semaphore_signal(barrier, inc=1, device_id=peer, device_id_type=MESH)

    count = [0]
    started = []

    def send(src, dst, device):
        n = count[0]
        count[0] += 1
        copy = pltpu.make_async_remote_copy(
            src_ref=src, dst_ref=dst, send_sem=send_sems.at[n], recv_sem=recv_sems.at[n],
            device_id=device, device_id_type=MESH,
        )
        copy.start()
        started.append(copy)
        return copy

    def arrive(copies):
        for copy in copies:
            copy.wait_recv()

    block = vol[...].reshape(256, 128)
    edges[...] = mm(t["edge"][...], block).astype(bf16)
    first_half = filt1[...].astype(bf16)
    wide_first = mm(first_half, t["widen"][...]).astype(bf16)
    bias1_col = row_to_column(bias1[...])
    bias2_col = row_to_column(bias2[...])
    second_half = filt2[...].astype(bf16)

    pl.semaphore_wait(barrier, len(peers))

    has_left, has_right = gx > 0, gx < GX - 1
    has_front, has_back = gz > 0, gz < GZ - 1
    has_below, has_above = gy > 0, gy < GY - 1

    def send_ring(wide_src, wide_dst, deep_src, deep_dst, corner_src, corner_dst):
        copies = []
        for a in range(2):
            dx = 1 if a == 0 else -1
            copies.append(send(wide_src(a), wide_dst.at[a], shifted(dx, 0, 0)))
        for b in range(2):
            dz = 1 if b == 0 else -1
            copies.append(send(deep_src(b), deep_dst.at[b], shifted(0, 0, dz)))
        for a in range(2):
            for b in range(2):
                copies.append(
                    send(corner_src(a, b), corner_dst.at[a * 2 + b], shifted(1 if a == 0 else -1, 0, 1 if b == 0 else -1))
                )
        return copies

    def send_columns(src, dst):
        return [send(src, dst.at[0], shifted(0, 1, 0)), send(src, dst.at[1], shifted(0, -1, 0))]

    def columns_in(dst):
        return jnp.concatenate([kept(has_below, dst[0]), kept(has_above, dst[1])], axis=0)

    def edge_rows(b):
        return edges.at[pl.ds(16, 16)] if b == 0 else edges.at[pl.ds(0, 16)]

    copies = send_ring(
        lambda a: vol.at[:, 3] if a == 0 else vol.at[:, 0], wide_in,
        edge_rows, deep_in, lambda a, b: edge_rows(b), corner_in,
    )

    turn = mm(second_half, t["ident"][...], TN).astype(bf16)
    for m in range(13):
        low = turn[64 * m:64 * m + 32, :128].astype(f32)
        high = turn[64 * m + 32:64 * m + 64, 128:].astype(f32)
        turned[:, 128 * m:128 * m + 128] = (low + high).astype(bf16)
    turned[:, 1664:1792] = turn[832:864, :128]
    spread_cot = mm(cot[...], t["spread"][...]) * 0.125

    arrive(copies)
    edge_flags = (has_left, has_right)
    deep_flags = (has_front, has_back)
    pieces = [block]
    for a in range(2):
        pieces.append(kept(edge_flags[a], wide_in[a]).reshape(64, 128))
    for b in range(2):
        pieces.append(kept(deep_flags[b], deep_in[b]))
    for a in range(2):
        for b in range(2):
            pieces.append(kept(jnp.logical_and(edge_flags[a], deep_flags[b]), corner_in[a * 2 + b]))
    rows = mm(t["place"][...], jnp.concatenate(pieces, axis=0)).astype(bf16)
    col1[...] = mm(t["pick1"][...], rows, NT).astype(bf16)
    copies = send_columns(col1, col1_in)
    inner = mm(rows, t["shift1"][...])
    arrive(copies)
    full = inner + mm(columns_in(col1_in), t["put1"][...], TN)
    third = [full[:, 128 * k:128 * k + 128].reshape(64, 8, 128) for k in range(3)]
    rolled = [pltpu.roll(piece, 4, axis=1) for piece in third]
    sub = lax.broadcasted_iota(jnp.int32, (64, 8, 128), 1)
    upper = sub < 4
    ones = jnp.where(sub == 4, 1.0, 0.0)
    even_tile = jnp.concatenate(
        [jnp.where(upper, third[0], rolled[1]), jnp.where(upper, third[2], ones)], axis=1
    )
    odd_tile = jnp.concatenate(
        [jnp.where(upper, rolled[0], third[1]), jnp.where(upper, rolled[2], ones)], axis=1
    )
    xs[:, 0] = even_tile.astype(bf16)
    xs[:, 1] = odd_tile.astype(bf16)

    def cols1(w, half_d):
        def at(i, dp, parity):
            return xs[(w + i) * 9 + dp, parity]

        one = [at(i, half_d + j // 2, j % 2) for i in range(3) for j in range(3)]
        two = [at(i, half_d + (j + 1) // 2, (j + 1) % 2) for i in range(3) for j in range(3)]
        return jnp.concatenate(
            [jnp.concatenate(one, axis=0), jnp.concatenate(two, axis=0)], axis=1
        )

    def forward1(pd, carry):
        for pw in range(2):
            part = None
            for w in (2 * pw, 2 * pw + 1):
                pre = mm(wide_first, cols1(w, pd)) + bias1_col
                pre1[w, pd] = pre
                act = leaky(pre)
                act = act[:, :128] + act[:, 128:]
                part = act if part is None else part + act
            part = (part + pltpu.roll(part, 127, axis=1)) * 0.125
            summed[pw, pd] = part.astype(bf16)
        return carry

    lax.fori_loop(0, 8, forward1, 0)
    pooled_val = (
        mm(summed[:, 0:4].reshape(256, 128), t["even"][0:128])
        + mm(summed[:, 4:8].reshape(256, 128), t["even"][128:256])
    ).astype(bf16)
    pooled[...] = pooled_val.reshape(2, 4, 32, 128)

    def assemble(own, wide, deep, corner, v, n):
        left = [kept(edge_flags[a], wide[a]) for a in range(2)]
        v[0:4] = left[0]
        v[4:8] = own[0]
        v[8:12] = own[1]
        v[12:16] = left[1]
        low = lax.broadcasted_iota(jnp.int32, (n, 128), 1) < 64
        for wp in range(4):
            if wp == 0 or wp == 3:
                a = 0 if wp == 0 else 1
                near = left[a]
                far = [
                    kept(jnp.logical_and(edge_flags[a], deep_flags[b]), corner[a * 2 + b]) for b in range(2)
                ]
            else:
                near = own[wp - 1]
                far = [kept(deep_flags[b], deep[b, wp - 1]) for b in range(2)]
            v[16 + wp] = jnp.where(low, near[3].astype(f32), far[0].astype(f32)).astype(bf16)
            v[20 + wp] = jnp.where(low, far[1].astype(f32), near[0].astype(f32)).astype(bf16)

    def halo(own, wide, deep, corner, v, col, col_in, out, n, flipped, meanwhile):
        copies = send_ring(
            lambda a: own.at[1 - a], wide,
            lambda b: own.at[:, 3 if b == 0 else 0], deep,
            lambda a, b: own.at[1 - a, 3 if b == 0 else 0], corner,
        )
        result = meanwhile()
        arrive(copies)
        assemble(own, wide, deep, corner, v, n)
        main = v[0:16].reshape(16 * n, 128)
        side = v[16:24].reshape(8 * n, 128)
        col[:, 0:16 * n] = mm(t["pick2"][...], main, NT).astype(bf16)
        col[:, 16 * n:24 * n] = mm(t["pick2s"][...], side, NT).astype(bf16)
        copies = send_columns(col, col_in)
        inner = jnp.concatenate([mm(main, t["shift2"][...]), mm(side, t["swapped"][...])], axis=0)
        arrive(copies)
        full = inner + mm(columns_in(col_in), t["put2"][...], TN)
        for k in range(3):
            place = 2 - k if flipped else k
            piece = full[:, 128 * k:128 * k + 128].astype(bf16).reshape(24, n, 128)
            out[:, place * n:place * n + n, :] = piece
        return result

    def tile(wp, dp):
        if dp == 0:
            return 16 + wp
        if dp == 5:
            return 20 + wp
        return wp * 4 + dp - 1

    halo(pooled, wide2, deep2, corner2, v2, col2, col2_in, ys, 32, False, lambda: None)

    def cols2(w, dq, extra):
        taps = [ys[tile(w + i, dq + j)] for i in range(3) for j in range(3)]
        return jnp.concatenate(taps + extra, axis=0)

    feat_sum = [None, None]
    for dq in range(4):
        cols = jnp.concatenate([cols2(0, dq, []), cols2(1, dq, [])], axis=1)
        pre = mm(second_half, cols) + bias2_col
        act = leaky(pre)
        act = act[:, :128] + act[:, 128:]
        pair = dq // 2
        feat_sum[pair] = act if feat_sum[pair] is None else feat_sum[pair] + act
        cot_here = spread_cot[:, 128 * pair:128 * pair + 128]
        err = (jnp.concatenate([cot_here, cot_here], axis=1) * slope(pre)).astype(bf16)
        errs[0, dq] = err[:, :128]
        errs[1, dq] = err[:, 128:]

    def second_half_grads():
        ends = [
            ((part + pltpu.roll(part, 127, axis=1)) * 0.125).astype(bf16) for part in feat_sum
        ]
        feat[...] = (mm(ends[0], t["gather"][0:128]) + mm(ends[1], t["gather"][128:256])).astype(bf16)
        ones_rows = [jnp.ones((32, 128), bf16)]
        grad2 = None
        for dq in range(4):
            cols = jnp.concatenate([cols2(0, dq, ones_rows), cols2(1, dq, ones_rows)], axis=1)
            err = jnp.concatenate([errs[0, dq], errs[1, dq]], axis=1)
            part = mm(err, cols, NT)
            grad2 = part if grad2 is None else grad2 + part
        for l in range(7):
            grads[l * 64:l * 64 + 64] = grad2[:, 128 * l:128 * l + 128]

    halo(errs, wide3, deep3, corner3, v3, col3, col3_in, fs, 64, True, second_half_grads)

    for dq in range(4):
        def cols3(w):
            taps = [fs[tile(w + 2 - i, dq + 2 - j)] for i in range(3) for j in range(3)]
            return jnp.concatenate(taps + [jnp.zeros((64, 128), bf16)], axis=0)

        cols = jnp.concatenate([cols3(0), cols3(1)], axis=1)
        pe = mm(turned[...], cols).astype(bf16)
        both = mm(jnp.concatenate([pe[:, :128], pe[:, 128:]], axis=0), t["twice"][...]) * 0.125
        for w in range(2):
            perr[w, dq] = both[32 * w:32 * w + 32, :128]
            perr[w, dq + 4] = both[32 * w:32 * w + 32, 128:]

    def backward1(pd, acc):
        for w in range(4):
            here = perr[w // 2, pd]
            err = (jnp.concatenate([here, here], axis=1) * slope(pre1[w, pd])).astype(bf16)
            acc = acc + mm(err, cols1(w, pd), NT)
        return acc

    grad1 = lax.fori_loop(0, 8, backward1, jnp.zeros((32, 144), f32))
    grads[448:480] = grad1[:, :128]
    grads[480:512] = jnp.concatenate([grad1[:, 128:144], jnp.zeros((32, 112), f32)], axis=1)

    def part(ref, index, size):
        return ref.at[pl.ds(pl.multiple_of(index * size, size), size)]

    n1, n2, n3 = 256, 256 // NX, 256 // NX // GY
    copy = send(part(grads, 1 - core, n1), core_in, sibling)
    copy.wait_recv()
    red1[...] = part(grads, core, n1)[...] + core_in[...]
    copies = [send(part(red1, x_peer(r)[0], n2), x_in.at[r - 1], x_peer(r)[1]) for r in range(1, NX)]
    arrive(copies)
    acc = part(red1, xc, n2)[...]
    for r in range(1, NX):
        acc = acc + x_in[r - 1]
    red2[...] = acc
    copies = [send(part(red2, y_peer(r)[0], n3), y_in.at[r - 1], y_peer(r)[1]) for r in range(1, GY)]
    arrive(copies)
    acc = part(red2, gy, n3)[...]
    for r in range(1, GY):
        acc = acc + y_in[r - 1]
    red3[...] = acc
    z_in[zc] = acc
    copies = [send(red3, z_in.at[zc], z_peer(r)) for r in range(1, NZ)]
    arrive(copies)
    acc = z_in[0]
    for r in range(1, NZ):
        acc = acc + z_in[r]
    mine = part(total, (core * NX + xc) * GY + gy, n3)
    mine[...] = acc
    copies = [send(mine, mine, y_peer(r)[1]) for r in range(1, GY)]
    arrive(copies)
    mine = part(total, core * NX + xc, n2)
    copies = [send(mine, mine, x_peer(r)[1]) for r in range(1, NX)]
    arrive(copies)
    mine = part(total, core, n1)
    copy = send(mine, mine, sibling)
    copy.wait_recv()

    sums2 = jnp.concatenate([total[l * 64:l * 64 + 64] for l in range(7)], axis=1)
    step2[...] = filt2[...] - learn_rate * sums2[:, :864]
    off2[...] = bias2[...] - learn_rate * column_to_row(sums2[:, 864:865])
    sums1 = jnp.concatenate([total[448:480], total[480:512]], axis=1)[:, :144]
    narrow = sum(mm(piece, t["narrow"][...]) for piece in split3(sums1))
    step1[...] = filt1[...] - learn_rate * narrow
    off1[...] = bias1[...] - learn_rate * column_to_row(sums1[:, 12:13])

    for copy in started:
        copy.wait_send()


def shards(volume, first_filters, first_bias, second_filters, second_bias, cotangent):
    GX, GY, GZ = lax.axis_size("gx"), lax.axis_size("gy"), lax.axis_size("gz")
    NX = 4 if GZ >= 8 else 2
    NZ = (GX // 2) * (GZ // NX)
    n2, n3 = 256 // NX, 256 // NX // GY
    table = tables()
    operands = [
        volume, first_filters, first_bias.reshape(1, 32), second_filters, second_bias.reshape(1, 64),
        cotangent.reshape(64, 128),
    ] + [jnp.asarray(table[name]) for name in TABLE_NAMES]
    sems = 30 + 1 + 2 * (NX - 1) + 2 * (GY - 1) + (NZ - 1) + 1
    V = pltpu.VMEM
    out = pl.pallas_call(
        functools.partial(kernel, (GX, GY, GZ, NX)),
        out_shape=(
            jax.ShapeDtypeStruct((64, 128), bf16),
            jax.ShapeDtypeStruct((32, 108), f32),
            jax.ShapeDtypeStruct((1, 32), f32),
            jax.ShapeDtypeStruct((64, 864), f32),
            jax.ShapeDtypeStruct((1, 64), f32),
        ),
        in_specs=[pl.BlockSpec(memory_space=pltpu.VMEM)] * len(operands),
        out_specs=[pl.BlockSpec(memory_space=pltpu.VMEM)] * 5,
        scratch_shapes=[
            V((32, 128), bf16), V((2, 4, 16, 128), bf16), V((2, 16, 128), bf16), V((4, 16, 128), bf16),
            V((16, 512), bf16), V((2, 16, 512), bf16), V((64, 2, 16, 128), bf16), V((4, 8, 32, 256), f32),
            V((2, 8, 32, 128), bf16),
            V((2, 4, 32, 128), bf16), V((2, 4, 32, 128), bf16), V((2, 2, 32, 128), bf16), V((4, 32, 128), bf16),
            V((24, 32, 128), bf16), V((16, 768), bf16), V((2, 16, 768), bf16), V((24, 96, 128), bf16),
            V((2, 4, 64, 128), bf16), V((2, 4, 64, 128), bf16), V((2, 2, 64, 128), bf16), V((4, 64, 128), bf16),
            V((24, 64, 128), bf16), V((16, 1536), bf16), V((2, 16, 1536), bf16), V((24, 192, 128), bf16),
            V((32, 1792), bf16), V((2, 8, 32, 128), f32),
            V((512, 128), f32), V((256, 128), f32), V((256, 128), f32), V((NX - 1, n2, 128), f32),
            V((n2, 128), f32), V((GY - 1, n3, 128), f32), V((n3, 128), f32), V((NZ, n3, 128), f32),
            V((512, 128), f32),
            pltpu.SemaphoreType.DMA((sems,)), pltpu.SemaphoreType.DMA((sems,)),
        ],
        compiler_params=pltpu.CompilerParams(
            collective_id=0, has_side_effects=True, vmem_limit_bytes=48 * 2**20
        ),
    )(*operands)
    features, stepped_first, offset_first, stepped_second, offset_second = out
    return (
        features.reshape(64, 1, 4, 32), stepped_first, offset_first.reshape(32), stepped_second,
        offset_second.reshape(64),
    )


def solution(mesh):
    return jax.shard_map(
        shards,
        mesh=mesh,
        in_specs=(P(None, "gx", "gz", "gy"), P(), P(), P(), P(), P(None, "gx", "gz", "gy")),
        out_specs=(P(None, "gx", "gz", "gy"), P(), P(), P(), P()),
        check_vma=False,
    )
```

time: 425 us -> 89 us (0.21)
  waiting for transfers between devices: 105 us -> 0 us
  local copies, waits for them, and re-layouts: 118 us -> 19.8 us
  blocking collectives: 79.8 us -> 0 us
  Pallas kernels: 0 us -> 67.5 us
  starting transfers between devices: 51.1 us -> 0 us
  other arithmetic: 43.3 us -> 0 us
  between operations: 14.4 us -> 0.71 us
  matrix products: 10.1 us -> 0 us
    psum x1 -> x0, waiting for transfers between devices: 79.8 us -> none  [shards(): lax.psum((first_grad, first_bias_grad, second_grad, second_bias_grad), ('...]
    psum x1 -> x0, blocking collectives: 79.8 us -> none  [shards(): lax.psum((first_grad, first_bias_grad, second_grad, second_bias_grad), ('...]
    pallas_call x0 -> x1, Pallas kernels: none -> 67.5 us  [shards(): pl.pallas_call(functools.partial(kernel, (GX, GY, GZ, NX)), out_shape=(ja...]
    ppermute x18 -> x0, starting transfers between devices: 51.1 us -> none  [the longest x9 37.4 us: extended(): lax.ppermute(tail, axis, [(i, (i + 1) % count) for i in range(ends)])]
    unnamed x89 -> x48, local copies, waits for them, and re-layouts: 49.3 us -> 18.2 us
    ppermute x18 -> x0, waiting for transfers between devices: 25 us -> none  [the longest x9 23.6 us: extended(): lax.ppermute(head, axis, [((i + 1) % count, i) for i in range(ends)])]
    reshape x4 -> x1, local copies, waits for them, and re-layouts: 20.7 us -> 0.87 us  [shards(): cotangent.reshape(64, 128)]
    unnamed x20 -> x0, other arithmetic: 17.4 us -> none
  transfers between devices with their start and end apart: 19 -> 0, of which waited for: 9 -> 0; matrix products, arithmetic and copies ran while one was open for 21% -> 0% of each run, Pallas kernels for 0% -> 0%
where the time goes in v1:
time: 89 us; the launch traced here: 88 us
  Pallas kernels  67.5 us (76%)
  local copies, waits for them, and re-layouts  19.8 us (22%)
    pallas_call x1, Pallas kernels, shards(): pl.pallas_call(functools.partial(kernel, (GX, GY, GZ, NX)), out_shape=(ja...  67.5 us
    unnamed x48, local copies, waits for them, and re-layouts  18.2 us

profile of v1, /device:TPU:1, one launch (start us, length us, event | category | flops | bytes accessed | tf_op | source)
XLA Modules:
  0.0 88.0 jit_solution(12757999918893029515)
XLA Ops:
  0.6 0.0 copy-start.16
  0.6 0.0 copy-start.6
  0.7 0.9 copy.30.refs_5_
  1.5 0.0 copy-done.16
  1.5 0.0 copy-done.6
  1.6 0.0 copy-start
  1.6 1.0 %copy-done = bf16[512,480]{1,0:T(8,128)(2,1)S(1)} copy-done((bf16[512,480]{1,0:T(8,128)(2,1)S(1)}, bf16[512,480]{1,0:T(8,128)(2,1)}, u32[]{:S(2)}) %copy-start) | copy-done | bytes 491544
  2.6 0.9 %copy-done.1 = f32[64,864]{1,0:T(8,128)S(1)} copy-done((f32[64,864]{1,0:T(8,128)S(1)}, f32[64,864]{1,0:T(8,128)}, u32[]{:S(2)}) %copy-start.1) | copy-done | bytes 221208
  3.5 0.9 %copy-done.2 = bf16[128,384]{1,0:T(8,128)(2,1)S(1)} copy-done((bf16[128,384]{1,0:T(8,128)(2,1)S(1)}, bf16[128,384]{1,0:T(8,128)(2,1)}, u32[]{:S(2)}) %copy-start.2) | copy-done | bytes 98328
  4.4 0.9 %copy-done.3 = bf16[128,384]{1,0:T(8,128)(2,1)S(1)} copy-done((bf16[128,384]{1,0:T(8,128)(2,1)S(1)}, bf16[128,384]{1,0:T(8,128)(2,1)}, u32[]{:S(2)}) %copy-start.3) | copy-done | bytes 98328
  5.3 0.9 %copy-done.4 = bf16[128,384]{1,0:T(8,128)(2,1)S(1)} copy-done((bf16[128,384]{1,0:T(8,128)(2,1)S(1)}, bf16[128,384]{1,0:T(8,128)(2,1)}, u32[]{:S(2)}) %copy-start.4) | copy-done | bytes 98328
  6.2 0.8 copy-done.5
  7.1 0.8 copy-done.7
  7.9 0.8 copy-done.8
  8.7 0.8 copy-done.9
  9.6 0.8 copy-done.10
  10.4 0.8 copy-done.11
  11.2 0.8 copy-done.12
  11.9 0.7 copy-done.13
  12.7 0.7 copy-done.14
  13.4 0.7 copy-done.15
  14.1 0.7 copy-done.17
  14.8 0.7 copy-done.18
  15.5 0.7 copy-done.19
  16.2 0.7 copy-done.20
  16.8 0.7 copy-done.21
  17.5 67.5 %shard_map.254 = (bf16[64,128]{1,0:T(8,128)(2,1)S(1)}, f32[32,108]{1,0:T(8,128)S(1)}, f32[1,32]{1,0:T(1,128)S(1)}, f32[64,864]{1,0:T(8,128)S(1)}, f32[1,64]{1,0:T(1,128)S(1)}) custom-call(bf16[4,4,16,128]{3,2,1,0:T(8,128)(2,1)S(1)} %copy-done.5, f32[32,108]{1,0:T(8,128)S(1)} %copy-done.15, f32[1,32]{1,0:T(1,128)S(1)} %bitcast.6, f32[64,864]{1,0:T(8,128)S(1)} %copy-done.1, ...), custom_call_target="tpu_custom_call" | custom-call | tf_op jit(solution)/shard_map/pallas_call | solution.py:488
  85.0 0.7 copy.31
  85.7 0.6 copy.36
  86.3 0.5 copy.37
  86.8 0.7 copy.38
  87.5 0.5 copy.39
  (19 shorter events, 0.0 us)
Async XLA Ops:
  0.6 0.9 %copy-start.16 = (bf16[32,256]{1,0:T(8,128)(2,1)S(1)}, bf16[32,256]{1,0:T(8,128)(2,1)}, u32[]{:S(2)}) copy-start(bf16[32,256]{1,0:T(8,128)(2,1)} %constant.34.clone.refs_6_) | copy-start | bytes 49156
  0.6 0.9 %copy-start.6 = (bf16[256,128]{1,0:T(8,128)(2,1)S(1)}, bf16[256,128]{1,0:T(8,128)(2,1)}, u32[]{:S(2)}) copy-start(bf16[256,128]{1,0:T(8,128)(2,1)} %constant.44.clone.refs_16_) | copy-start | bytes 196612
  1.6 1.0 %copy-start = (bf16[512,480]{1,0:T(8,128)(2,1)S(1)}, bf16[512,480]{1,0:T(8,128)(2,1)}, u32[]{:S(2)}) copy-start(bf16[512,480]{1,0:T(8,128)(2,1)} %constant.35.clone.refs_7_) | copy-start | bytes 1474564
  2.6 0.9 %copy-start.1 = (f32[64,864]{1,0:T(8,128)S(1)}, f32[64,864]{1,0:T(8,128)}, u32[]{:S(2)}) copy-start(f32[64,864]{1,0:T(8,128)} %refs_3_.1) | copy-start | bytes 663556
  3.5 0.9 %copy-start.2 = (bf16[128,384]{1,0:T(8,128)(2,1)S(1)}, bf16[128,384]{1,0:T(8,128)(2,1)}, u32[]{:S(2)}) copy-start(bf16[128,384]{1,0:T(8,128)(2,1)} %constant.36.clone.refs_8_) | copy-start | bytes 294916
  4.4 0.9 %copy-start.3 = (bf16[128,384]{1,0:T(8,128)(2,1)S(1)}, bf16[128,384]{1,0:T(8,128)(2,1)}, u32[]{:S(2)}) copy-start(bf16[128,384]{1,0:T(8,128)(2,1)} %constant.39.clone.refs_11_) | copy-start | bytes 294916
  5.3 0.9 %copy-start.4 = (bf16[128,384]{1,0:T(8,128)(2,1)S(1)}, bf16[128,384]{1,0:T(8,128)(2,1)}, u32[]{:S(2)}) copy-start(bf16[128,384]{1,0:T(8,128)(2,1)} %constant.40.clone.refs_12_) | copy-start | bytes 294916
  6.2 0.8 copy-start.5
  7.1 0.8 copy-start.7
  7.9 0.8 copy-start.8
  8.7 0.8 copy-start.9
  9.6 0.8 copy-start.10
  10.4 0.8 copy-start.11
  11.2 0.8 copy-start.12
  11.9 0.7 copy-start.13
  12.7 0.7 copy-start.14
  13.4 0.7 copy-start.15
  14.1 0.7 copy-start.17
  14.8 0.7 copy-start.18
  15.5 0.7 copy-start.19
  16.2 0.7 copy-start.20
  16.8 0.7 copy-start.21

commit v2 on v1

--- a/solution.py
+++ b/solution.py
@@ -23,10 +23,6 @@
 
 
 def tables():
-    edge = np.zeros((32, 256))
-    for r in range(16):
-        edge[r, r * 16] = 1
-        edge[16 + r, r * 16 + 15] = 1
     place = np.zeros((512, 480))
     for wp in range(6):
         for dp in range(18):
@@ -81,24 +77,56 @@
         for h in range(128):
             twice[half * 64 + h // 2, half * 128 + h] = 1
     spread = np.zeros((128, 256))
-    gather = np.zeros((256, 128))
+    collect = np.zeros((256, 128))
     for dc in range(4):
         for hc in range(32):
             for t in range(2):
                 spread[dc * 32 + hc, (dc % 2) * 128 + (dc // 2) * 64 + 2 * hc + t] = 1
-            gather[(dc % 2) * 128 + (dc // 2) * 64 + 2 * hc, dc * 32 + hc] = 1
+            collect[(dc % 2) * 128 + dc * 32 + hc, (dc // 2) * 64 + 2 * hc] = 1
     widen = np.zeros((108, 144))
+    narrow = np.zeros((144, 128))
     for q in range(108):
         widen[q, (q // 12) * 16 + q % 12] = 1
+        narrow[(q // 12) * 16 + q % 12, q] = 1
+    narrow[12, 108] = 1
     ident = np.zeros((64, 256))
     for o in range(64):
         ident[o, o] = ident[o, 128 + 64 + o] = 1
     every = dict(
-        edge=edge, place=place, shift1=shift1, pick1=pick1, put1=put1, shift2=shift2, swapped=swapped,
-        pick2=pick2, pick2s=pick2s, put2=put2, even=even, twice=twice, spread=spread, gather=gather,
-        widen=widen, narrow=widen.T, ident=ident,
-    )
-    return {name: value.astype(jnp.bfloat16) for name, value in every.items()}
+        place=place, shift1=shift1, pick1=pick1, put1=put1, shift2=shift2, swapped=swapped,
+        pick2=pick2, pick2s=pick2s, put2=put2, even=even, twice=twice, spread=spread, collect=collect,
+        widen=widen, narrow=narrow, ident=ident,
+    )
+    return every
+
+
+TABLE = {}
+
+
+def packed_table():
+    parts, row = [], 0
+    for name, value in tables().items():
+        rows, lanes = value.shape
+        wide = np.zeros((-(-rows // 16) * 16, 512))
+        wide[:rows, :lanes] = value
+        TABLE[name] = (row, rows, lanes)
+        row += wide.shape[0]
+        parts.append(wide)
+    return np.concatenate(parts).astype(jnp.bfloat16)
+
+
+PACKED = packed_table()
+
+
+class Rows:
+    def __init__(self, ref, name):
+        self.ref = ref
+        self.row, self.rows, self.lanes = TABLE[name]
+
+    def __getitem__(self, key):
+        if key is Ellipsis:
+            return self.ref[self.row:self.row + self.rows, :self.lanes]
+        return self.ref[self.row + key.start:self.row + key.stop, :self.lanes]
 
 
 def row_to_column(row):
@@ -132,27 +160,27 @@
     return high, mid, (rest - mid.astype(f32)).astype(bf16)
 
 
-TABLE_NAMES = (
-    "edge", "place", "shift1", "pick1", "put1", "shift2", "swapped", "pick2", "pick2s", "put2",
-    "even", "twice", "spread", "gather", "widen", "narrow", "ident",
-)
-
-
 def kernel(sizes, *refs):
     GX, GY, GZ, NX = sizes
     ZL = GZ // NX
     ZH = GX // 2
     NZ = ZH * ZL
-    vol, filt1, bias1, filt2, bias2, cot = refs[:6]
-    t = dict(zip(TABLE_NAMES, refs[6:6 + len(TABLE_NAMES)]))
-    refs = refs[6 + len(TABLE_NAMES):]
-    feat, step1, off1, step2, off2 = refs[:5]
+    far = refs[:7]
+    refs = refs[7:]
+    far_out = refs[:5]
     (
         edges, wide_in, deep_in, corner_in, col1, col1_in, xs, pre1, summed,
         pooled, wide2, deep2, corner2, v2, col2, col2_in, ys,
         errs, wide3, deep3, corner3, v3, col3, col3_in, fs, turned, perr,
-        grads, core_in, red1, x_in, red2, y_in, red3, z_in, total, send_sems, recv_sems,
+        grads, core_in, red1, x_in, red2, y_in, red3, z_in, total,
+        one, one_core, one_x, one_y, one_z, one_total, send_sems, recv_sems, vol, filt1, bias1, filt2, bias2, cot, packed, in_sems,
+        feat, step1, off1, step2, off2, out_sems,
     ) = refs[5:]
+    near = (vol, filt1, bias1, filt2, bias2, cot, packed)
+    fetches = [pltpu.make_async_copy(a, b, in_sems.at[n]) for n, (a, b) in enumerate(zip(far, near))]
+    for fetch in fetches:
+        fetch.start()
+    t = {name: Rows(packed, name) for name in TABLE}
 
     gx, gy, gz = lax.axis_index("gx"), lax.axis_index("gy"), lax.axis_index("gz")
     core, zh = lax.rem(gx, 2), lax.div(gx, 2)
@@ -200,18 +228,22 @@
         started.append(copy)
         return copy
 
+    def put_out(n):
+        copy = pltpu.make_async_copy((feat, step1, off1, step2, off2)[n], far_out[n], out_sems.at[n])
+        copy.start()
+        return copy
+
     def arrive(copies):
         for copy in copies:
             copy.wait_recv()
 
+    row = lax.broadcasted_iota(jnp.int32, (32, 256), 0)
+    column = lax.broadcasted_iota(jnp.int32, (32, 256), 1)
+    wanted = jnp.where(row < 16, row * 16, row * 16 - 241)
+    edge = jnp.where(column == wanted, 1.0, 0.0).astype(bf16)
+    fetches[0].wait()
     block = vol[...].reshape(256, 128)
-    edges[...] = mm(t["edge"][...], block).astype(bf16)
-    first_half = filt1[...].astype(bf16)
-    wide_first = mm(first_half, t["widen"][...]).astype(bf16)
-    bias1_col = row_to_column(bias1[...])
-    bias2_col = row_to_column(bias2[...])
-    second_half = filt2[...].astype(bf16)
-
+    edges[...] = mm(edge, block).astype(bf16)
     pl.semaphore_wait(barrier, len(peers))
 
     has_left, has_right = gx > 0, gx < GX - 1
@@ -247,13 +279,21 @@
         edge_rows, deep_in, lambda a, b: edge_rows(b), corner_in,
     )
 
+    for fetch in fetches[1:]:
+        fetch.wait()
+    first_half = filt1[...].astype(bf16)
+    wide_first = mm(first_half, t["widen"][...]).astype(bf16)
+    bias1_col = row_to_column(bias1[...])
+    bias2_col = row_to_column(bias2[...])
+    second_half = filt2[...].astype(bf16)
+
     turn = mm(second_half, t["ident"][...], TN).astype(bf16)
     for m in range(13):
         low = turn[64 * m:64 * m + 32, :128].astype(f32)
         high = turn[64 * m + 32:64 * m + 64, 128:].astype(f32)
         turned[:, 128 * m:128 * m + 128] = (low + high).astype(bf16)
     turned[:, 1664:1792] = turn[832:864, :128]
-    spread_cot = mm(cot[...], t["spread"][...]) * 0.125
+    spread_cot = mm(cot[...], t["spread"][...], TN) * 0.125
 
     arrive(copies)
     edge_flags = (has_left, has_right)
@@ -336,7 +376,7 @@
             v[16 + wp] = jnp.where(low, near[3].astype(f32), far[0].astype(f32)).astype(bf16)
             v[20 + wp] = jnp.where(low, far[1].astype(f32), near[0].astype(f32)).astype(bf16)
 
-    def halo(own, wide, deep, corner, v, col, col_in, out, n, flipped, meanwhile):
+    def halo(own, wide, deep, corner, v, col, col_in, out, n, flipped, meanwhile, between):
         copies = send_ring(
             lambda a: own.at[1 - a], wide,
             lambda b: own.at[:, 3 if b == 0 else 0], deep,
@@ -350,6 +390,7 @@
         col[:, 0:16 * n] = mm(t["pick2"][...], main, NT).astype(bf16)
         col[:, 16 * n:24 * n] = mm(t["pick2s"][...], side, NT).astype(bf16)
         copies = send_columns(col, col_in)
+        result = between(result)
         inner = jnp.concatenate([mm(main, t["shift2"][...]), mm(side, t["swapped"][...])], axis=0)
         arrive(copies)
         full = inner + mm(columns_in(col_in), t["put2"][...], TN)
@@ -366,7 +407,7 @@
             return 20 + wp
         return wp * 4 + dp - 1
 
-    halo(pooled, wide2, deep2, corner2, v2, col2, col2_in, ys, 32, False, lambda: None)
+    halo(pooled, wide2, deep2, corner2, v2, col2, col2_in, ys, 32, False, lambda: None, lambda a: a)
 
     def cols2(w, dq, extra):
         taps = [ys[tile(w + i, dq + j)] for i in range(3) for j in range(3)]
@@ -387,20 +428,82 @@
 
     def second_half_grads():
         ends = [
-            ((part + pltpu.roll(part, 127, axis=1)) * 0.125).astype(bf16) for part in feat_sum
+            ((both + pltpu.roll(both, 127, axis=1)) * 0.125).astype(bf16) for both in feat_sum
         ]
-        feat[...] = (mm(ends[0], t["gather"][0:128]) + mm(ends[1], t["gather"][128:256])).astype(bf16)
+        feat[...] = (mm(t["collect"][0:128], ends[0], NT) + mm(t["collect"][128:256], ends[1], NT)).astype(bf16)
         ones_rows = [jnp.ones((32, 128), bf16)]
         grad2 = None
         for dq in range(4):
             cols = jnp.concatenate([cols2(0, dq, ones_rows), cols2(1, dq, ones_rows)], axis=1)
             err = jnp.concatenate([errs[0, dq], errs[1, dq]], axis=1)
-            part = mm(err, cols, NT)
-            grad2 = part if grad2 is None else grad2 + part
+            piece = mm(err, cols, NT)
+            grad2 = piece if grad2 is None else grad2 + piece
         for l in range(7):
             grads[l * 64:l * 64 + 64] = grad2[:, 128 * l:128 * l + 128]
-
-    halo(errs, wide3, deep3, corner3, v3, col3, col3_in, fs, 64, True, second_half_grads)
+        grads[448:512] = jnp.zeros((64, 128), f32)
+        return put_out(0), send(part(grads, 1 - core, n1), core_in, sibling)
+
+    def part(ref, index, size):
+        return ref.at[pl.ds(pl.multiple_of(index * size, size), size)]
+
+    n1, n2, n3 = 256, 256 // NX, 256 // NX // GY
+
+    def sum_core(copy):
+        copy.wait_recv()
+        red1[...] = part(grads, core, n1)[...] + core_in[...]
+        return [send(part(red1, x_peer(r)[0], n2), x_in.at[r - 1], x_peer(r)[1]) for r in range(1, NX)]
+
+    def sum_x(copies):
+        arrive(copies)
+        acc = part(red1, xc, n2)[...]
+        for r in range(1, NX):
+            acc = acc + x_in[r - 1]
+        red2[...] = acc
+        return [send(part(red2, y_peer(r)[0], n3), y_in.at[r - 1], y_peer(r)[1]) for r in range(1, GY)]
+
+    def sum_y(copies):
+        arrive(copies)
+        acc = part(red2, gy, n3)[...]
+        for r in range(1, GY):
+            acc = acc + y_in[r - 1]
+        red3[...] = acc
+        z_in[zc] = acc
+        return [send(red3, z_in.at[zc], z_peer(r)) for r in range(1, NZ)]
+
+    def sum_z(copies):
+        arrive(copies)
+        acc = z_in[0]
+        for r in range(1, NZ):
+            acc = acc + z_in[r]
+        mine = part(total, (core * NX + xc) * GY + gy, n3)
+        mine[...] = acc
+        return [send(mine, mine, y_peer(r)[1]) for r in range(1, GY)]
+
+    def gather_x(copies):
+        arrive(copies)
+        mine = part(total, core * NX + xc, n2)
+        return [send(mine, mine, x_peer(r)[1]) for r in range(1, NX)]
+
+    def gather_core(copies):
+        arrive(copies)
+        mine = part(total, core, n1)
+        return send(mine, mine, sibling)
+
+    def everyone(value, slots, index, devices):
+        slots[index] = value
+        return [send(slots.at[index], slots.at[index], device) for device in devices]
+
+    def summed_slots(copies, slots):
+        arrive(copies)
+        acc = slots[0]
+        for n in range(1, slots.shape[0]):
+            acc = acc + slots[n]
+        return acc
+
+    feat_out, copies2 = halo(
+        errs, wide3, deep3, corner3, v3, col3, col3_in, fs, 64, True, second_half_grads,
+        lambda a: (a[0], sum_core(a[1])),
+    )
 
     for dq in range(4):
         def cols3(w):
@@ -414,6 +517,8 @@
             perr[w, dq] = both[32 * w:32 * w + 32, :128]
             perr[w, dq + 4] = both[32 * w:32 * w + 32, 128:]
 
+    copies2 = sum_x(copies2)
+
     def backward1(pd, acc):
         for w in range(4):
             here = perr[w // 2, pd]
@@ -422,55 +527,45 @@
         return acc
 
     grad1 = lax.fori_loop(0, 8, backward1, jnp.zeros((32, 144), f32))
-    grads[448:480] = grad1[:, :128]
-    grads[480:512] = jnp.concatenate([grad1[:, 128:144], jnp.zeros((32, 112), f32)], axis=1)
-
-    def part(ref, index, size):
-        return ref.at[pl.ds(pl.multiple_of(index * size, size), size)]
-
-    n1, n2, n3 = 256, 256 // NX, 256 // NX // GY
-    copy = send(part(grads, 1 - core, n1), core_in, sibling)
-    copy.wait_recv()
-    red1[...] = part(grads, core, n1)[...] + core_in[...]
-    copies = [send(part(red1, x_peer(r)[0], n2), x_in.at[r - 1], x_peer(r)[1]) for r in range(1, NX)]
-    arrive(copies)
-    acc = part(red1, xc, n2)[...]
-    for r in range(1, NX):
-        acc = acc + x_in[r - 1]
-    red2[...] = acc
-    copies = [send(part(red2, y_peer(r)[0], n3), y_in.at[r - 1], y_peer(r)[1]) for r in range(1, GY)]
-    arrive(copies)
-    acc = part(red2, gy, n3)[...]
-    for r in range(1, GY):
-        acc = acc + y_in[r - 1]
-    red3[...] = acc
-    z_in[zc] = acc
-    copies = [send(red3, z_in.at[zc], z_peer(r)) for r in range(1, NZ)]
-    arrive(copies)
-    acc = z_in[0]
-    for r in range(1, NZ):
-        acc = acc + z_in[r]
-    mine = part(total, (core * NX + xc) * GY + gy, n3)
-    mine[...] = acc
-    copies = [send(mine, mine, y_peer(r)[1]) for r in range(1, GY)]
-    arrive(copies)
-    mine = part(total, core * NX + xc, n2)
-    copies = [send(mine, mine, x_peer(r)[1]) for r in range(1, NX)]
-    arrive(copies)
-    mine = part(total, core, n1)
-    copy = send(mine, mine, sibling)
-    copy.wait_recv()
-
+    one[...] = sum(mm(piece, t["narrow"][...]) for piece in split3(grad1))
+    copies1 = send(part(one, 1 - core, 16), one_core, sibling)
+    copies2 = sum_y(copies2)
+    copies1.wait_recv()
+    copies1 = everyone(part(one, core, 16)[...] + one_core[...], one_x, xc, [x_peer(r)[1] for r in range(1, NX)])
+    copies2 = sum_z(copies2)
+    copies1 = everyone(summed_slots(copies1, one_x), one_y, gy, [y_peer(r)[1] for r in range(1, GY)])
+    copies2 = gather_x(copies2)
+    copies1 = everyone(summed_slots(copies1, one_y), one_z, zc, [z_peer(r) for r in range(1, NZ)])
+    copy2 = gather_core(copies2)
+    mine = part(one_total, core, 16)
+    mine[...] = summed_slots(copies1, one_z)
+    copy1 = send(mine, mine, sibling)
+
+    copy2.wait_recv()
     sums2 = jnp.concatenate([total[l * 64:l * 64 + 64] for l in range(7)], axis=1)
     step2[...] = filt2[...] - learn_rate * sums2[:, :864]
     off2[...] = bias2[...] - learn_rate * column_to_row(sums2[:, 864:865])
-    sums1 = jnp.concatenate([total[448:480], total[480:512]], axis=1)[:, :144]
-    narrow = sum(mm(piece, t["narrow"][...]) for piece in split3(sums1))
-    step1[...] = filt1[...] - learn_rate * narrow
-    off1[...] = bias1[...] - learn_rate * column_to_row(sums1[:, 12:13])
+    outs = [put_out(3), put_out(4)]
+    copy1.wait_recv()
+    sums1 = one_total[...]
+    step1[...] = filt1[...] - learn_rate * sums1[:, :108]
+    off1[...] = bias1[...] - learn_rate * column_to_row(sums1[:, 108:109])
+    outs += [put_out(1), put_out(2)]
 
     for copy in started:
         copy.wait_send()
+    feat_out.wait()
+    for out in outs:
+        out.wait()
+
+
+def hand_on(*refs):
+    sems = refs[10]
+    copies = [pltpu.make_async_copy(refs[n], refs[5 + n], sems.at[n]) for n in range(5)]
+    for copy in copies:
+        copy.start()
+    for copy in copies:
+        copy.wait()
 
 
 def shards(volume, first_filters, first_bias, second_filters, second_bias, cotangent):
@@ -478,24 +573,24 @@
     NX = 4 if GZ >= 8 else 2
     NZ = (GX // 2) * (GZ // NX)
     n2, n3 = 256 // NX, 256 // NX // GY
-    table = tables()
     operands = [
         volume, first_filters, first_bias.reshape(1, 32), second_filters, second_bias.reshape(1, 64),
-        cotangent.reshape(64, 128),
-    ] + [jnp.asarray(table[name]) for name in TABLE_NAMES]
-    sems = 30 + 1 + 2 * (NX - 1) + 2 * (GY - 1) + (NZ - 1) + 1
+        cotangent.transpose(1, 2, 3, 0).reshape(128, 64), jnp.asarray(PACKED),
+    ]
+    sems = 30 + 4 + 3 * (NX - 1) + 3 * (GY - 1) + 2 * (NZ - 1)
     V = pltpu.VMEM
+    results = (
+        jax.ShapeDtypeStruct((128, 64), bf16),
+        jax.ShapeDtypeStruct((32, 108), f32),
+        jax.ShapeDtypeStruct((1, 32), f32),
+        jax.ShapeDtypeStruct((64, 864), f32),
+        jax.ShapeDtypeStruct((1, 64), f32),
+    )
     out = pl.pallas_call(
         functools.partial(kernel, (GX, GY, GZ, NX)),
-        out_shape=(
-            jax.ShapeDtypeStruct((64, 128), bf16),
-            jax.ShapeDtypeStruct((32, 108), f32),
-            jax.ShapeDtypeStruct((1, 32), f32),
-            jax.ShapeDtypeStruct((64, 864), f32),
-            jax.ShapeDtypeStruct((1, 64), f32),
-        ),
-        in_specs=[pl.BlockSpec(memory_space=pltpu.VMEM)] * len(operands),
-        out_specs=[pl.BlockSpec(memory_space=pltpu.VMEM)] * 5,
+        out_shape=results,
+        in_specs=[pl.BlockSpec(memory_space=pltpu.HBM)] * len(operands),
+        out_specs=[pl.BlockSpec(memory_space=pltpu.HBM)] * 5,
         scratch_shapes=[
             V((32, 128), bf16), V((2, 4, 16, 128), bf16), V((2, 16, 128), bf16), V((4, 16, 128), bf16),
             V((16, 512), bf16), V((2, 16, 512), bf16), V((64, 2, 16, 128), bf16), V((4, 8, 32, 256), f32),
@@ -508,15 +603,29 @@
             V((512, 128), f32), V((256, 128), f32), V((256, 128), f32), V((NX - 1, n2, 128), f32),
             V((n2, 128), f32), V((GY - 1, n3, 128), f32), V((n3, 128), f32), V((NZ, n3, 128), f32),
             V((512, 128), f32),
+            V((32, 128), f32), V((16, 128), f32), V((NX, 16, 128), f32), V((GY, 16, 128), f32),
+            V((NZ, 16, 128), f32), V((32, 128), f32),
             pltpu.SemaphoreType.DMA((sems,)), pltpu.SemaphoreType.DMA((sems,)),
+        ] + [V(a.shape, a.dtype) for a in operands] + [
+            pltpu.SemaphoreType.DMA((len(operands),)),
+        ] + [V(a.shape, a.dtype) for a in results] + [
+            pltpu.SemaphoreType.DMA((5,)),
         ],
         compiler_params=pltpu.CompilerParams(
-            collective_id=0, has_side_effects=True, vmem_limit_bytes=48 * 2**20
+            collective_id=0, has_side_effects=True, vmem_limit_bytes=62 * 2**20
         ),
     )(*operands)
+    out = pl.pallas_call(
+        hand_on,
+        out_shape=results,
+        in_specs=[pl.BlockSpec(memory_space=pltpu.HBM)] * 5,
+        out_specs=[pl.BlockSpec(memory_space=pltpu.HBM)] * 5,
+        scratch_shapes=[pltpu.SemaphoreType.DMA((5,))],
+        compiler_params=pltpu.CompilerParams(vmem_limit_bytes=62 * 2**20),
+    )(*out)
     features, stepped_first, offset_first, stepped_second, offset_second = out
     return (
-        features.reshape(64, 1, 4, 32), stepped_first, offset_first.reshape(32), stepped_second,
+        features.reshape(1, 4, 32, 64).transpose(3, 0, 1, 2), stepped_first, offset_first.reshape(32), stepped_second,
         offset_second.reshape(64),
     )
 

time: 89 us -> 73.1 us (0.82)
  local copies, waits for them, and re-layouts: 19.8 us -> 0 us
  Pallas kernels: 67.5 us -> 72.3 us
    unnamed x48 -> x0, local copies, waits for them, and re-layouts: 18.2 us -> none
    pallas_call x1 -> x2, Pallas kernels: 67.5 us -> 72.3 us  [the longest x1 62.7 us: shards(): pl.pallas_call(functools.partial(kernel, (GX, GY, GZ, NX)), out_shape=res...]
where the time goes in v2:
time: 73.1 us; the launch traced here: 73 us
  Pallas kernels  72.3 us (99%)
    pallas_call x1, Pallas kernels, shards(): pl.pallas_call(functools.partial(kernel, (GX, GY, GZ, NX)), out_shape=res...  62.7 us
    pallas_call x1, Pallas kernels, shards(): pl.pallas_call(hand_on, out_shape=results, in_specs=[pl.BlockSpec(memory_...  9.62 us

profile of v2, /device:TPU:1, one launch (start us, length us, event | category | flops | bytes accessed | tf_op | source)
XLA Modules:
  0.0 73.0 jit_solution(9856558820366882288)
XLA Ops:
  0.6 62.7 %shard_map.110 = (bf16[128,64]{1,0:T(8,128)(2,1)}, f32[32,108]{1,0:T(8,128)}, f32[1,32]{1,0:T(1,128)}, f32[64,864]{1,0:T(8,128)}, f32[1,64]{1,0:T(1,128)}) custom-call(bf16[4,4,16,128]{3,2,1,0:T(8,128)(2,1)} %refs_0_.1, f32[32,108]{1,0:T(8,128)} %refs_1_.1, f32[1,32]{1,0:T(1,128)} %bitcast.11, f32[64,864]{1,0:T(8,128)} %refs_3_.1, f32[1,64]{1,0:T(1,128)} %bitcast.12, ...), custom_call_target="tpu_custom_call" | custom-call | tf_op jit(solution)/shard_map/pallas_call | solution.py:589
  63.4 9.6 %shard_map.111 = (bf16[128,64]{1,0:T(8,128)(2,1)}, f32[32,108]{1,0:T(8,128)}, f32[1,32]{1,0:T(1,128)}, f32[64,864]{1,0:T(8,128)}, f32[1,64]{1,0:T(1,128)}) custom-call(bf16[128,64]{1,0:T(8,128)(2,1)} %get-tuple-element.15.refs_0_, f32[32,108]{1,0:T(8,128)} %get-tuple-element.16.refs_1_, f32[1,32]{1,0:T(1,128)} %get-tuple-element.17.refs_2_, ...), custom_call_target="tpu_custom_call" | custom-call | tf_op jit(solution)/shard_map/pallas_call | solution.py:618

commit v3 on v2

--- a/solution.py
+++ b/solution.py
@@ -46,11 +46,18 @@
         shift1[l, 128 + l] = 1
         if l < 127:
             shift1[l + 1, 256 + l] = 1
-    pick1 = np.zeros((16, 128))
-    pick1[0, 0] = pick1[1, 127] = 1
-    put1 = np.zeros((32, 384))
-    put1[1, 0] = 1
-    put1[16, 256 + 127] = 1
+    order1 = np.zeros((1152, 128))
+    for wp in range(6):
+        for dp in range(18):
+            a, b = (wp > 0) + (wp > 4), (dp > 0) + (dp > 16)
+            w, d = (3, wp - 1, 0)[a], (15, dp - 1, 0)[b]
+            order1[(a * 3 + b) * 128 + w * 16 + d, wp * 18 + dp] = 1
+    four = np.zeros((128, 512))
+    for q in range(512):
+        four[q // 4, q] = 1
+    put1 = np.zeros((32, 256))
+    for ch in range(4):
+        put1[ch * 2 + 1, 0] = put1[16 + ch * 2, 255] = 1
     shift2 = np.zeros((128, 384))
     swapped = np.zeros((128, 384))
     for l in range(128):
@@ -60,14 +67,22 @@
                 s += l - l % 64
                 shift2[s, k * 128 + l] = 1
                 swapped[(s + 64) % 128, k * 128 + l] = 1
-    pick2 = np.zeros((16, 128))
-    pick2s = np.zeros((16, 128))
-    for r, l in enumerate((0, 63, 64, 127)):
-        pick2[r, l] = 1
-        pick2s[r, (l + 64) % 128] = 1
-    put2 = np.zeros((32, 384))
-    put2[1, 0] = put2[3, 64] = 1
-    put2[16, 256 + 63] = put2[18, 256 + 127] = 1
+    ends = (0, 63, 64, 127)
+    pick2 = np.zeros((16, 512))
+    for dq in range(4):
+        for n, l in enumerate(ends):
+            pick2[dq * 4 + n, dq * 128 + l] = 1
+    put2 = np.zeros((96, 1536))
+    for dp in range(6):
+        if dp == 0:
+            near = ((0, 3, 1), (1, 3, 0))
+        elif dp == 5:
+            near = ((1, 0, 1), (2, 0, 0))
+        else:
+            near = ((1, dp - 1, 0), (1, dp - 1, 1))
+        for half, (dz, dq, there) in enumerate(near):
+            put2[dz * 16 + dq * 4 + 2 * there + 1, dp * 256 + 64 * half] = 1
+            put2[48 + dz * 16 + dq * 4 + 2 * there, dp * 256 + 128 + 64 * half + 63] = 1
     even = np.zeros((256, 128))
     for half in range(2):
         for h in range(64):
@@ -93,8 +108,8 @@
     for o in range(64):
         ident[o, o] = ident[o, 128 + 64 + o] = 1
     every = dict(
-        place=place, shift1=shift1, pick1=pick1, put1=put1, shift2=shift2, swapped=swapped,
-        pick2=pick2, pick2s=pick2s, put2=put2, even=even, twice=twice, spread=spread, collect=collect,
+        place=place, shift1=shift1, order1=order1, four=four, put1=put1, shift2=shift2, swapped=swapped,
+        pick2=pick2, put2=put2, even=even, twice=twice, spread=spread, collect=collect,
         widen=widen, narrow=narrow, ident=ident,
     )
     return every
@@ -107,8 +122,9 @@
     parts, row = [], 0
     for name, value in tables().items():
         rows, lanes = value.shape
-        wide = np.zeros((-(-rows // 16) * 16, 512))
+        wide = np.zeros((-(-rows // 16) * 16, -(-lanes // 512) * 512))
         wide[:rows, :lanes] = value
+        wide = np.concatenate(np.split(wide, wide.shape[1] // 512, axis=1))
         TABLE[name] = (row, rows, lanes)
         row += wide.shape[0]
         parts.append(wide)
@@ -124,6 +140,12 @@
         self.row, self.rows, self.lanes = TABLE[name]
 
     def __getitem__(self, key):
+        if self.lanes > 512:
+            step = -(-self.rows // 16) * 16
+            return jnp.concatenate(
+                [self.ref[self.row + n * step:self.row + n * step + self.rows, :] for n in range(self.lanes // 512)],
+                axis=1,
+            )
         if key is Ellipsis:
             return self.ref[self.row:self.row + self.rows, :self.lanes]
         return self.ref[self.row + key.start:self.row + key.stop, :self.lanes]
@@ -204,9 +226,9 @@
         p = lax.rem(zc + r, NZ)
         return (2 * lax.div(p, ZL) + core, gy, lax.rem(p, ZL) * NX + xc)
 
-    ring = [(dx, dz) for dx in (-1, 0, 1) for dz in (-1, 0, 1) if (dx, dz) != (0, 0)]
-    peers = [shifted(dx, 0, dz) for dx, dz in ring]
-    peers += [shifted(0, -1, 0), shifted(0, 1, 0), sibling]
+    square = [(dx, dz) for dx in (-1, 0, 1) for dz in (-1, 0, 1)]
+    peers = [shifted(dx, 0, dz) for dx, dz in square if (dx, dz) != (0, 0)]
+    peers += [shifted(dx, dy, dz) for dx, dz in square for dy in (-1, 1)]
     peers += [x_peer(r)[1] for r in range(1, NX)]
     peers += [y_peer(r)[1] for r in range(1, GY)]
     peers += [z_peer(r) for r in range(1, NZ)]
@@ -266,10 +288,27 @@
         return copies
 
     def send_columns(src, dst):
-        return [send(src, dst.at[0], shifted(0, 1, 0)), send(src, dst.at[1], shifted(0, -1, 0))]
-
-    def columns_in(dst):
-        return jnp.concatenate([kept(has_below, dst[0]), kept(has_above, dst[1])], axis=0)
+        copies = []
+        for dx, dz in square:
+            for side in range(2):
+                dy = 1 if side == 0 else -1
+                copies.append(send(src, dst.at[side, 1 - dx, 1 - dz], shifted(dx, dy, dz)))
+        return copies
+
+    def columns_in(dst, dx):
+        rows = []
+        for side in range(2):
+            for dz in (-1, 0, 1):
+                flag = (has_below, has_above)[side]
+                if dx:
+                    flag = jnp.logical_and(flag, edge_flags[(dx + 1) // 2])
+                if dz:
+                    flag = jnp.logical_and(flag, deep_flags[(dz + 1) // 2])
+                rows.append(kept(flag, dst[side, dx + 1, dz + 1]))
+        return rows
+
+    edge_flags = (has_left, has_right)
+    deep_flags = (has_front, has_back)
 
     def edge_rows(b):
         return edges.at[pl.ds(16, 16)] if b == 0 else edges.at[pl.ds(0, 16)]
@@ -279,6 +318,15 @@
         edge_rows, deep_in, lambda a, b: edge_rows(b), corner_in,
     )
 
+    row = lax.broadcasted_iota(jnp.int32, (16, 512), 0)
+    column = lax.broadcasted_iota(jnp.int32, (16, 512), 1)
+    wanted = jnp.where(row < 8, lax.div(row, 2) * 128 + lax.rem(row, 2) * 127, -1)
+    pick1 = jnp.where(column == wanted, 1.0, 0.0).astype(bf16)
+    ends = sum(
+        mm(pick1[:, 128 * ch:128 * ch + 128], vol[ch].reshape(64, 128), NT) for ch in range(4)
+    )
+    col1[...] = jnp.concatenate([ends, jnp.zeros((16, 64), f32)], axis=1).astype(bf16)
+    copies_c = send_columns(col1, col1_in)
     for fetch in fetches[1:]:
         fetch.wait()
     first_half = filt1[...].astype(bf16)
@@ -296,8 +344,6 @@
     spread_cot = mm(cot[...], t["spread"][...], TN) * 0.125
 
     arrive(copies)
-    edge_flags = (has_left, has_right)
-    deep_flags = (has_front, has_back)
     pieces = [block]
     for a in range(2):
         pieces.append(kept(edge_flags[a], wide_in[a]).reshape(64, 128))
@@ -307,12 +353,22 @@
         for b in range(2):
             pieces.append(kept(jnp.logical_and(edge_flags[a], deep_flags[b]), corner_in[a * 2 + b]))
     rows = mm(t["place"][...], jnp.concatenate(pieces, axis=0)).astype(bf16)
-    col1[...] = mm(t["pick1"][...], rows, NT).astype(bf16)
-    copies = send_columns(col1, col1_in)
     inner = mm(rows, t["shift1"][...])
-    arrive(copies)
-    full = inner + mm(columns_in(col1_in), t["put1"][...], TN)
-    third = [full[:, 128 * k:128 * k + 128].reshape(64, 8, 128) for k in range(3)]
+    arrive(copies_c)
+    columns = [columns_in(col1_in, dx) for dx in (-1, 0, 1)]
+    sides = [
+        jnp.concatenate([columns[a][side * 3 + b] for a in range(3) for b in range(3)], axis=1)
+        for side in range(2)
+    ]
+    ordered = mm(jnp.concatenate(sides, axis=0), t["order1"][...]).astype(bf16)
+    ordered = mm(ordered, t["four"][...])
+    row = lax.broadcasted_iota(jnp.int32, (32, 512), 0)
+    column = lax.broadcasted_iota(jnp.int32, (32, 512), 1)
+    same = lax.rem(lax.div(row, 2), 8) == lax.rem(column, 4)
+    ordered = jnp.where(same, ordered, 0.0).astype(bf16)
+    ends = mm(ordered, t["put1"][...], TN)
+    full = [inner[:, :128] + ends[:, :128], inner[:, 128:256], inner[:, 256:] + ends[:, 128:]]
+    third = [piece.reshape(64, 8, 128) for piece in full]
     rolled = [pltpu.roll(piece, 4, axis=1) for piece in third]
     sub = lax.broadcasted_iota(jnp.int32, (64, 8, 128), 1)
     upper = sub < 4
@@ -382,22 +438,35 @@
             lambda b: own.at[:, 3 if b == 0 else 0], deep,
             lambda a, b: own.at[1 - a, 3 if b == 0 else 0], corner,
         )
+        pick = t["pick2"][...]
+        ends = sum(
+            mm(pick[:, 128 * dq:128 * dq + 128], own[:, dq].reshape(2 * n, 128), NT) for dq in range(4)
+        )
+        if n < 64:
+            ends = jnp.concatenate([ends, jnp.zeros((16, 128 - 2 * n), f32)], axis=1)
+        col[...] = ends.astype(bf16)
+        copies_c = send_columns(col, col_in)
         result = meanwhile()
         arrive(copies)
         assemble(own, wide, deep, corner, v, n)
         main = v[0:16].reshape(16 * n, 128)
         side = v[16:24].reshape(8 * n, 128)
-        col[:, 0:16 * n] = mm(t["pick2"][...], main, NT).astype(bf16)
-        col[:, 16 * n:24 * n] = mm(t["pick2s"][...], side, NT).astype(bf16)
-        copies = send_columns(col, col_in)
+        inner = jnp.concatenate([mm(main, t["shift2"][...]), mm(side, t["swapped"][...])], axis=0)
         result = between(result)
-        inner = jnp.concatenate([mm(main, t["shift2"][...]), mm(side, t["swapped"][...])], axis=0)
-        arrive(copies)
-        full = inner + mm(columns_in(col_in), t["put2"][...], TN)
-        for k in range(3):
-            place = 2 - k if flipped else k
-            piece = full[:, 128 * k:128 * k + 128].astype(bf16).reshape(24, n, 128)
-            out[:, place * n:place * n + n, :] = piece
+        arrive(copies_c)
+        put = t["put2"][...]
+        edge = [mm(jnp.concatenate(columns_in(col_in, dx), axis=0), put, TN) for dx in (-1, 0, 1)]
+        for wp in range(4):
+            far, w = ((0, 1), (1, 0), (1, 1), (2, 0))[wp]
+            for dp in range(6):
+                number = tile(wp, dp)
+                for k in range(3):
+                    piece = inner[number * n:number * n + n, 128 * k:128 * k + 128]
+                    if k != 1:
+                        lane = dp * 256 + 64 * k
+                        piece = piece + edge[far][w * n:w * n + n, lane:lane + 128]
+                    place = 2 - k if flipped else k
+                    out[number, place * n:place * n + n, :] = piece.astype(bf16)
         return result
 
     def tile(wp, dp):
@@ -560,11 +629,15 @@
 
 
 def hand_on(*refs):
-    sems = refs[10]
-    copies = [pltpu.make_async_copy(refs[n], refs[5 + n], sems.at[n]) for n in range(5)]
-    for copy in copies:
+    ins, outs, spots, in_sems, out_sems = refs[:5], refs[5:10], refs[10:15], refs[15], refs[16]
+    reads = [pltpu.make_async_copy(ins[n], spots[n], in_sems.at[n]) for n in range(5)]
+    writes = [pltpu.make_async_copy(spots[n], outs[n], out_sems.at[n]) for n in range(5)]
+    for copy in reads:
         copy.start()
-    for copy in copies:
+    for n in (3, 0, 1, 2, 4):
+        reads[n].wait()
+        writes[n].start()
+    for copy in writes:
         copy.wait()
 
 
@@ -577,7 +650,7 @@
         volume, first_filters, first_bias.reshape(1, 32), second_filters, second_bias.reshape(1, 64),
         cotangent.transpose(1, 2, 3, 0).reshape(128, 64), jnp.asarray(PACKED),
     ]
-    sems = 30 + 4 + 3 * (NX - 1) + 3 * (GY - 1) + 2 * (NZ - 1)
+    sems = 78 + 4 + 3 * (NX - 1) + 3 * (GY - 1) + 2 * (NZ - 1)
     V = pltpu.VMEM
     results = (
         jax.ShapeDtypeStruct((128, 64), bf16),
@@ -593,12 +666,12 @@
         out_specs=[pl.BlockSpec(memory_space=pltpu.HBM)] * 5,
         scratch_shapes=[
             V((32, 128), bf16), V((2, 4, 16, 128), bf16), V((2, 16, 128), bf16), V((4, 16, 128), bf16),
-            V((16, 512), bf16), V((2, 16, 512), bf16), V((64, 2, 16, 128), bf16), V((4, 8, 32, 256), f32),
+            V((16, 128), bf16), V((2, 3, 3, 16, 128), bf16), V((64, 2, 16, 128), bf16), V((4, 8, 32, 256), f32),
             V((2, 8, 32, 128), bf16),
             V((2, 4, 32, 128), bf16), V((2, 4, 32, 128), bf16), V((2, 2, 32, 128), bf16), V((4, 32, 128), bf16),
-            V((24, 32, 128), bf16), V((16, 768), bf16), V((2, 16, 768), bf16), V((24, 96, 128), bf16),
+            V((24, 32, 128), bf16), V((16, 128), bf16), V((2, 3, 3, 16, 128), bf16), V((24, 96, 128), bf16),
             V((2, 4, 64, 128), bf16), V((2, 4, 64, 128), bf16), V((2, 2, 64, 128), bf16), V((4, 64, 128), bf16),
-            V((24, 64, 128), bf16), V((16, 1536), bf16), V((2, 16, 1536), bf16), V((24, 192, 128), bf16),
+            V((24, 64, 128), bf16), V((16, 128), bf16), V((2, 3, 3, 16, 128), bf16), V((24, 192, 128), bf16),
             V((32, 1792), bf16), V((2, 8, 32, 128), f32),
             V((512, 128), f32), V((256, 128), f32), V((256, 128), f32), V((NX - 1, n2, 128), f32),
             V((n2, 128), f32), V((GY - 1, n3, 128), f32), V((n3, 128), f32), V((NZ, n3, 128), f32),
@@ -620,7 +693,8 @@
         out_shape=results,
         in_specs=[pl.BlockSpec(memory_space=pltpu.HBM)] * 5,
         out_specs=[pl.BlockSpec(memory_space=pltpu.HBM)] * 5,
-        scratch_shapes=[pltpu.SemaphoreType.DMA((5,))],
+        scratch_shapes=[V(a.shape, a.dtype) for a in results]
+        + [pltpu.SemaphoreType.DMA((5,)), pltpu.SemaphoreType.DMA((5,))],
         compiler_params=pltpu.CompilerParams(vmem_limit_bytes=62 * 2**20),
     )(*out)
     features, stepped_first, offset_first, stepped_second, offset_second = out

time: 73.1 us -> 62.2 us (0.85)
  Pallas kernels: 72.3 us -> 61.5 us
    pallas_call x1, Pallas kernels: 9.62 us -> 1.76 us  [shards(): pl.pallas_call(hand_on, out_shape=results, in_specs=[pl.BlockSpec(memory_...]
    pallas_call x1, Pallas kernels: 62.7 us -> 59.7 us  [shards(): pl.pallas_call(functools.partial(kernel, (GX, GY, GZ, NX)), out_shape=res...]
where the time goes in v3:
time: 62.2 us; the launch traced here: 62.1 us
  Pallas kernels  61.5 us (99%)
  between operations  0.64 us (1%)
    pallas_call x1, Pallas kernels, shards(): pl.pallas_call(functools.partial(kernel, (GX, GY, GZ, NX)), out_shape=res...  59.7 us
    pallas_call x1, Pallas kernels, shards(): pl.pallas_call(hand_on, out_shape=results, in_specs=[pl.BlockSpec(memory_...  1.76 us

profile of v3, /device:TPU:1, one launch (start us, length us, event | category | flops | bytes accessed | tf_op | source)
XLA Modules:
  0.0 62.1 jit_solution(13701111447910855521)
XLA Ops:
  0.6 59.7 %shard_map.110 = (bf16[128,64]{1,0:T(8,128)(2,1)}, f32[32,108]{1,0:T(8,128)}, f32[1,32]{1,0:T(1,128)}, f32[64,864]{1,0:T(8,128)}, f32[1,64]{1,0:T(1,128)}) custom-call(bf16[4,4,16,128]{3,2,1,0:T(8,128)(2,1)} %refs_0_.1, f32[32,108]{1,0:T(8,128)} %refs_1_.1, f32[1,32]{1,0:T(1,128)} %bitcast.11, f32[64,864]{1,0:T(8,128)} %refs_3_.1, f32[1,64]{1,0:T(1,128)} %bitcast.12, ...), custom_call_target="tpu_custom_call" | custom-call | tf_op jit(solution)/shard_map/pallas_call | solution.py:662
  60.3 1.8 %shard_map.111 = (bf16[128,64]{1,0:T(8,128)(2,1)}, f32[32,108]{1,0:T(8,128)}, f32[1,32]{1,0:T(1,128)}, f32[64,864]{1,0:T(8,128)}, f32[1,64]{1,0:T(1,128)}) custom-call(bf16[128,64]{1,0:T(8,128)(2,1)} %get-tuple-element.15.refs_0_, f32[32,108]{1,0:T(8,128)} %get-tuple-element.16.refs_1_, f32[1,32]{1,0:T(1,128)} %get-tuple-element.17.refs_2_, ...), custom_call_target="tpu_custom_call" | custom-call | tf_op jit(solution)/shard_map/pallas_call | solution.py:691

commit v4 on v3

--- a/solution.py
+++ b/solution.py
@@ -510,7 +510,7 @@
         for l in range(7):
             grads[l * 64:l * 64 + 64] = grad2[:, 128 * l:128 * l + 128]
         grads[448:512] = jnp.zeros((64, 128), f32)
-        return put_out(0), send(part(grads, 1 - core, n1), core_in, sibling)
+        return put_out(0), sum_core(send(part(grads, 1 - core, n1), core_in, sibling))
 
     def part(ref, index, size):
         return ref.at[pl.ds(pl.multiple_of(index * size, size), size)]
@@ -571,7 +571,7 @@
 
     feat_out, copies2 = halo(
         errs, wide3, deep3, corner3, v3, col3, col3_in, fs, 64, True, second_half_grads,
-        lambda a: (a[0], sum_core(a[1])),
+        lambda a: (a[0], sum_x(a[1])),
     )
 
     for dq in range(4):
@@ -586,7 +586,7 @@
             perr[w, dq] = both[32 * w:32 * w + 32, :128]
             perr[w, dq + 4] = both[32 * w:32 * w + 32, 128:]
 
-    copies2 = sum_x(copies2)
+    copies2 = sum_y(copies2)
 
     def backward1(pd, acc):
         for w in range(4):
@@ -598,7 +598,6 @@
     grad1 = lax.fori_loop(0, 8, backward1, jnp.zeros((32, 144), f32))
     one[...] = sum(mm(piece, t["narrow"][...]) for piece in split3(grad1))
     copies1 = send(part(one, 1 - core, 16), one_core, sibling)
-    copies2 = sum_y(copies2)
     copies1.wait_recv()
     copies1 = everyone(part(one, core, 16)[...] + one_core[...], one_x, xc, [x_peer(r)[1] for r in range(1, NX)])
     copies2 = sum_z(copies2)
@@ -606,15 +605,14 @@
     copies2 = gather_x(copies2)
     copies1 = everyone(summed_slots(copies1, one_y), one_z, zc, [z_peer(r) for r in range(1, NZ)])
     copy2 = gather_core(copies2)
-    mine = part(one_total, core, 16)
-    mine[...] = summed_slots(copies1, one_z)
-    copy1 = send(mine, mine, sibling)
-
     copy2.wait_recv()
     sums2 = jnp.concatenate([total[l * 64:l * 64 + 64] for l in range(7)], axis=1)
     step2[...] = filt2[...] - learn_rate * sums2[:, :864]
     off2[...] = bias2[...] - learn_rate * column_to_row(sums2[:, 864:865])
     outs = [put_out(3), put_out(4)]
+    mine = part(one_total, core, 16)
+    mine[...] = summed_slots(copies1, one_z)
+    copy1 = send(mine, mine, sibling)
     copy1.wait_recv()
     sums1 = one_total[...]
     step1[...] = filt1[...] - learn_rate * sums1[:, :108]

time: 62.2 us -> 59.3 us (0.953)
  Pallas kernels: 61.5 us -> 58.6 us
    pallas_call x1, Pallas kernels: 59.7 us -> 56.8 us  [shards(): pl.pallas_call(functools.partial(kernel, (GX, GY, GZ, NX)), out_shape=res...]
where the time goes in v4:
time: 59.3 us; the launch traced here: 59.2 us
  Pallas kernels  58.6 us (99%)
  between operations  0.64 us (1%)
    pallas_call x1, Pallas kernels, shards(): pl.pallas_call(functools.partial(kernel, (GX, GY, GZ, NX)), out_shape=res...  56.8 us
    pallas_call x1, Pallas kernels, shards(): pl.pallas_call(hand_on, out_shape=results, in_specs=[pl.BlockSpec(memory_...  1.76 us

profile of v4, /device:TPU:1, one launch (start us, length us, event | category | flops | bytes accessed | tf_op | source)
XLA Modules:
  0.0 59.2 jit_solution(3882329604383555300)
XLA Ops:
  0.6 56.8 %shard_map.110 = (bf16[128,64]{1,0:T(8,128)(2,1)}, f32[32,108]{1,0:T(8,128)}, f32[1,32]{1,0:T(1,128)}, f32[64,864]{1,0:T(8,128)}, f32[1,64]{1,0:T(1,128)}) custom-call(bf16[4,4,16,128]{3,2,1,0:T(8,128)(2,1)} %refs_0_.1, f32[32,108]{1,0:T(8,128)} %refs_1_.1, f32[1,32]{1,0:T(1,128)} %bitcast.11, f32[64,864]{1,0:T(8,128)} %refs_3_.1, f32[1,64]{1,0:T(1,128)} %bitcast.12, ...), custom_call_target="tpu_custom_call" | custom-call | tf_op jit(solution)/shard_map/pallas_call | solution.py:660
  57.4 1.8 %shard_map.111 = (bf16[128,64]{1,0:T(8,128)(2,1)}, f32[32,108]{1,0:T(8,128)}, f32[1,32]{1,0:T(1,128)}, f32[64,864]{1,0:T(8,128)}, f32[1,64]{1,0:T(1,128)}) custom-call(bf16[128,64]{1,0:T(8,128)(2,1)} %get-tuple-element.15.refs_0_, f32[32,108]{1,0:T(8,128)} %get-tuple-element.16.refs_1_, f32[1,32]{1,0:T(1,128)} %get-tuple-element.17.refs_2_, ...), custom_call_target="tpu_custom_call" | custom-call | tf_op jit(solution)/shard_map/pallas_call | solution.py:689

commit v5 on v4

--- a/solution.py
+++ b/solution.py
@@ -72,17 +72,22 @@
     for dq in range(4):
         for n, l in enumerate(ends):
             pick2[dq * 4 + n, dq * 128 + l] = 1
-    put2 = np.zeros((96, 1536))
-    for dp in range(6):
-        if dp == 0:
-            near = ((0, 3, 1), (1, 3, 0))
-        elif dp == 5:
-            near = ((1, 0, 1), (2, 0, 0))
-        else:
-            near = ((1, dp - 1, 0), (1, dp - 1, 1))
-        for half, (dz, dq, there) in enumerate(near):
-            put2[dz * 16 + dq * 4 + 2 * there + 1, dp * 256 + 64 * half] = 1
-            put2[48 + dz * 16 + dq * 4 + 2 * there, dp * 256 + 128 + 64 * half + 63] = 1
+    put2 = np.zeros((96, 2048))
+    for dq in range(-2, 6):
+        for half in range(2):
+            d = dq + 4 * half
+            dz = (d >= 0) + (d > 7)
+            there, row = (d % 8) // 4, (d % 4) * 4
+            put2[dz * 16 + row + 2 * there + 1, (dq + 2) * 256 + 64 * half] = 1
+            put2[48 + dz * 16 + row + 2 * there, (dq + 2) * 256 + 128 + 64 * half + 63] = 1
+    pick3 = np.zeros((32, 768))
+    put3 = np.zeros((64, 1536))
+    for dq in range(6):
+        for n, l in enumerate(ends):
+            pick3[dq * 4 + n, dq * 128 + l] = 1
+        for half in range(2):
+            put3[dq * 4 + 2 * half + 1, dq * 256 + 64 * half] = 1
+            put3[32 + dq * 4 + 2 * half, dq * 256 + 128 + 64 * half + 63] = 1
     even = np.zeros((256, 128))
     for half in range(2):
         for h in range(64):
@@ -91,12 +96,18 @@
     for half in range(2):
         for h in range(128):
             twice[half * 64 + h // 2, half * 128 + h] = 1
-    spread = np.zeros((128, 256))
+    spread = np.zeros((192, 512))
+    for dc in range(-1, 5):
+        for hc in range(32):
+            row = (128 if dc < 0 else 160 if dc > 3 else dc * 32) + hc
+            for t in range(2):
+                for half in range(2):
+                    kind = {0: 0, 1: 1, -1: 2, 2: 3}.get(dc - 2 * half)
+                    if kind is not None:
+                        spread[row, kind * 128 + half * 64 + 2 * hc + t] = 1
     collect = np.zeros((256, 128))
     for dc in range(4):
         for hc in range(32):
-            for t in range(2):
-                spread[dc * 32 + hc, (dc % 2) * 128 + (dc // 2) * 64 + 2 * hc + t] = 1
             collect[(dc % 2) * 128 + dc * 32 + hc, (dc // 2) * 64 + 2 * hc] = 1
     widen = np.zeros((108, 144))
     narrow = np.zeros((144, 128))
@@ -109,7 +120,7 @@
         ident[o, o] = ident[o, 128 + 64 + o] = 1
     every = dict(
         place=place, shift1=shift1, order1=order1, four=four, put1=put1, shift2=shift2, swapped=swapped,
-        pick2=pick2, put2=put2, even=even, twice=twice, spread=spread, collect=collect,
+        pick2=pick2, put2=put2, pick3=pick3, put3=put3, even=even, twice=twice, spread=spread, collect=collect,
         widen=widen, narrow=narrow, ident=ident,
     )
     return every
@@ -122,8 +133,11 @@
     parts, row = [], 0
     for name, value in tables().items():
         rows, lanes = value.shape
+        if name == "order1":
+            value = np.concatenate(np.split(value, 4), axis=1)
+            rows //= 4
         wide = np.zeros((-(-rows // 16) * 16, -(-lanes // 512) * 512))
-        wide[:rows, :lanes] = value
+        wide[:rows, :value.shape[1]] = value
         wide = np.concatenate(np.split(wide, wide.shape[1] // 512, axis=1))
         TABLE[name] = (row, rows, lanes)
         row += wide.shape[0]
@@ -139,11 +153,16 @@
         self.ref = ref
         self.row, self.rows, self.lanes = TABLE[name]
 
+    def folded(self):
+        return jnp.concatenate(
+            [self.ref[self.row:self.row + self.rows, 128 * n:128 * n + 128] for n in range(4)], axis=0
+        )
+
     def __getitem__(self, key):
         if self.lanes > 512:
             step = -(-self.rows // 16) * 16
             return jnp.concatenate(
-                [self.ref[self.row + n * step:self.row + n * step + self.rows, :] for n in range(self.lanes // 512)],
+                [self.ref[self.row + n * step:self.row + n * step + self.rows, :] for n in range(-(-self.lanes // 512))],
                 axis=1,
             )
         if key is Ellipsis:
@@ -192,8 +211,8 @@
     far_out = refs[:5]
     (
         edges, wide_in, deep_in, corner_in, col1, col1_in, xs, pre1, summed,
-        pooled, wide2, deep2, corner2, v2, col2, col2_in, ys,
-        errs, wide3, deep3, corner3, v3, col3, col3_in, fs, turned, perr,
+        wide_t, deep_t, corner_t, pooled, packs, wide2, deep2, corner2, v2, col2, col2_in, ys,
+        errs, col3, col3_in, fs, turned, perr,
         grads, core_in, red1, x_in, red2, y_in, red3, z_in, total,
         one, one_core, one_x, one_y, one_z, one_total, send_sems, recv_sems, vol, filt1, bias1, filt2, bias2, cot, packed, in_sems,
         feat, step1, off1, step2, off2, out_sems,
@@ -335,13 +354,17 @@
     bias2_col = row_to_column(bias2[...])
     second_half = filt2[...].astype(bf16)
 
+    copies_t = send_ring(
+        lambda a: cot, wide_t, lambda b: cot.at[96:128] if b == 0 else cot.at[0:32], deep_t,
+        lambda a, b: cot.at[96:128] if b == 0 else cot.at[0:32], corner_t,
+    )
+
     turn = mm(second_half, t["ident"][...], TN).astype(bf16)
     for m in range(13):
         low = turn[64 * m:64 * m + 32, :128].astype(f32)
         high = turn[64 * m + 32:64 * m + 64, 128:].astype(f32)
         turned[:, 128 * m:128 * m + 128] = (low + high).astype(bf16)
     turned[:, 1664:1792] = turn[832:864, :128]
-    spread_cot = mm(cot[...], t["spread"][...], TN) * 0.125
 
     arrive(copies)
     pieces = [block]
@@ -360,7 +383,7 @@
         jnp.concatenate([columns[a][side * 3 + b] for a in range(3) for b in range(3)], axis=1)
         for side in range(2)
     ]
-    ordered = mm(jnp.concatenate(sides, axis=0), t["order1"][...]).astype(bf16)
+    ordered = mm(jnp.concatenate(sides, axis=0), t["order1"].folded()).astype(bf16)
     ordered = mm(ordered, t["four"][...])
     row = lax.broadcasted_iota(jnp.int32, (32, 512), 0)
     column = lax.broadcasted_iota(jnp.int32, (32, 512), 1)
@@ -412,88 +435,96 @@
     ).astype(bf16)
     pooled[...] = pooled_val.reshape(2, 4, 32, 128)
 
-    def assemble(own, wide, deep, corner, v, n):
-        left = [kept(edge_flags[a], wide[a]) for a in range(2)]
-        v[0:4] = left[0]
-        v[4:8] = own[0]
-        v[8:12] = own[1]
-        v[12:16] = left[1]
-        low = lax.broadcasted_iota(jnp.int32, (n, 128), 1) < 64
-        for wp in range(4):
-            if wp == 0 or wp == 3:
-                a = 0 if wp == 0 else 1
-                near = left[a]
-                far = [
-                    kept(jnp.logical_and(edge_flags[a], deep_flags[b]), corner[a * 2 + b]) for b in range(2)
-                ]
-            else:
-                near = own[wp - 1]
-                far = [kept(deep_flags[b], deep[b, wp - 1]) for b in range(2)]
-            v[16 + wp] = jnp.where(low, near[3].astype(f32), far[0].astype(f32)).astype(bf16)
-            v[20 + wp] = jnp.where(low, far[1].astype(f32), near[0].astype(f32)).astype(bf16)
-
-    def halo(own, wide, deep, corner, v, col, col_in, out, n, flipped, meanwhile, between):
-        copies = send_ring(
-            lambda a: own.at[1 - a], wide,
-            lambda b: own.at[:, 3 if b == 0 else 0], deep,
-            lambda a, b: own.at[1 - a, 3 if b == 0 else 0], corner,
-        )
-        pick = t["pick2"][...]
-        ends = sum(
-            mm(pick[:, 128 * dq:128 * dq + 128], own[:, dq].reshape(2 * n, 128), NT) for dq in range(4)
-        )
-        if n < 64:
-            ends = jnp.concatenate([ends, jnp.zeros((16, 128 - 2 * n), f32)], axis=1)
-        col[...] = ends.astype(bf16)
-        copies_c = send_columns(col, col_in)
-        result = meanwhile()
-        arrive(copies)
-        assemble(own, wide, deep, corner, v, n)
-        main = v[0:16].reshape(16 * n, 128)
-        side = v[16:24].reshape(8 * n, 128)
-        inner = jnp.concatenate([mm(main, t["shift2"][...]), mm(side, t["swapped"][...])], axis=0)
-        result = between(result)
-        arrive(copies_c)
-        put = t["put2"][...]
-        edge = [mm(jnp.concatenate(columns_in(col_in, dx), axis=0), put, TN) for dx in (-1, 0, 1)]
-        for wp in range(4):
-            far, w = ((0, 1), (1, 0), (1, 1), (2, 0))[wp]
-            for dp in range(6):
-                number = tile(wp, dp)
-                for k in range(3):
-                    piece = inner[number * n:number * n + n, 128 * k:128 * k + 128]
-                    if k != 1:
-                        lane = dp * 256 + 64 * k
-                        piece = piece + edge[far][w * n:w * n + n, lane:lane + 128]
-                    place = 2 - k if flipped else k
-                    out[number, place * n:place * n + n, :] = piece.astype(bf16)
-        return result
-
-    def tile(wp, dp):
-        if dp == 0:
-            return 16 + wp
-        if dp == 5:
-            return 20 + wp
-        return wp * 4 + dp - 1
-
-    halo(pooled, wide2, deep2, corner2, v2, col2, col2_in, ys, 32, False, lambda: None, lambda a: a)
+    def turned_half(a):
+        return pltpu.roll(a.astype(f32), 64, axis=1)
+
+    low = lax.broadcasted_iota(jnp.int32, (32, 128), 1) < 64
+
+    def halves(a, b):
+        return jnp.where(low, a.astype(f32), b.astype(f32)).astype(bf16)
+
+    for w in range(2):
+        packs[0, w] = halves(turned_half(pooled[w, 2]), pooled[w, 3])
+        packs[1, w] = halves(pooled[w, 0], turned_half(pooled[w, 1]))
+    copies = send_ring(
+        lambda a: pooled, wide2, lambda b: packs.at[b], deep2, lambda a, b: packs.at[b], corner2
+    )
+    pick = t["pick2"][...]
+    ends = sum(
+        mm(pick[:, 128 * dq:128 * dq + 128], pooled[:, dq].reshape(64, 128), NT) for dq in range(4)
+    )
+    col2[...] = jnp.concatenate([ends, jnp.zeros((16, 64), f32)], axis=1).astype(bf16)
+    copies_c = send_columns(col2, col2_in)
+
+    arrive(copies_t)
+    spread_cot = []
+    for dx in (-1, 0, 1):
+        a = max(dx, 0)
+        beside = edge_flags[a]
+        if dx:
+            rows = [kept(beside, wide_t[a])]
+            rows += [kept(jnp.logical_and(beside, deep_flags[b]), corner_t[a * 2 + b]) for b in range(2)]
+        else:
+            rows = [cot[...]] + [kept(deep_flags[b], deep_t[b]) for b in range(2)]
+        spread_cot.append(mm(jnp.concatenate(rows, axis=0), t["spread"][...], TN) * 0.125)
+
+    arrive(copies)
+    for wp in range(6):
+        a, w = wp // 4, wp % 2
+        if wp in (2, 3):
+            near = [pooled[w, dq] for dq in range(4)]
+            front, back = (kept(deep_flags[b], deep2[b, w]) for b in range(2))
+        else:
+            near = [kept(edge_flags[a], wide2[a, w, dq]) for dq in range(4)]
+            front, back = (
+                kept(jnp.logical_and(edge_flags[a], deep_flags[b]), corner2[a * 2 + b, w]) for b in range(2)
+            )
+        for dq in range(4):
+            v2[wp * 6 + dq] = near[dq]
+        v2[wp * 6 + 4] = halves(front, turned_half(near[2]))
+        v2[wp * 6 + 5] = halves(turned_half(near[1]), back)
+        v2[36 + wp] = halves(near[3], front)
+        v2[42 + wp] = halves(back, near[0])
+    inner = jnp.concatenate(
+        [mm(v2[0:36].reshape(1152, 128), t["shift2"][...]), mm(v2[36:48].reshape(384, 128), t["swapped"][...])],
+        axis=0,
+    )
+    arrive(copies_c)
+    put = t["put2"][...]
+    edge = [mm(jnp.concatenate(columns_in(col2_in, dx), axis=0), put, TN) for dx in (-1, 0, 1)]
+    for wp in range(6):
+        for dp in range(8):
+            number = {0: wp * 6 + 4, 1: 36 + wp, 6: 42 + wp, 7: wp * 6 + 5}.get(dp, wp * 6 + dp - 2)
+            for k in range(3):
+                piece = inner[number * 32:number * 32 + 32, 128 * k:128 * k + 128]
+                if k != 1:
+                    lane = dp * 256 + 64 * k
+                    piece = piece + edge[wp // 2][(wp % 2) * 32:(wp % 2) * 32 + 32, lane:lane + 128]
+                ys[wp * 8 + dp, k * 32:k * 32 + 32, :] = piece.astype(bf16)
 
     def cols2(w, dq, extra):
-        taps = [ys[tile(w + i, dq + j)] for i in range(3) for j in range(3)]
+        taps = [ys[(w + i) * 8 + dq + j] for i in range(3) for j in range(3)]
         return jnp.concatenate(taps + extra, axis=0)
 
     feat_sum = [None, None]
-    for dq in range(4):
-        cols = jnp.concatenate([cols2(0, dq, []), cols2(1, dq, [])], axis=1)
-        pre = mm(second_half, cols) + bias2_col
-        act = leaky(pre)
-        act = act[:, :128] + act[:, 128:]
-        pair = dq // 2
-        feat_sum[pair] = act if feat_sum[pair] is None else feat_sum[pair] + act
-        cot_here = spread_cot[:, 128 * pair:128 * pair + 128]
-        err = (jnp.concatenate([cot_here, cot_here], axis=1) * slope(pre)).astype(bf16)
-        errs[0, dq] = err[:, :128]
-        errs[1, dq] = err[:, 128:]
+    for dq in range(6):
+        kind = {0: 2, 5: 3}.get(dq, (dq - 1) // 2)
+        for pair in ((1, 2), (0, 3)):
+            cols = jnp.concatenate([cols2(w, dq, []) for w in pair], axis=1)
+            pre = mm(second_half, cols) + bias2_col
+            if pair == (1, 2) and 0 < dq < 5:
+                act = leaky(pre)
+                act = act[:, :128] + act[:, 128:]
+                feat_sum[kind] = act if feat_sum[kind] is None else feat_sum[kind] + act
+            for n, w in enumerate(pair):
+                here = spread_cot[(w + 1) // 2][:, 128 * kind:128 * kind + 128]
+                errs[w, dq] = (here * slope(pre[:, 128 * n:128 * n + 128])).astype(bf16)
+
+    pick = t["pick3"][...]
+    col3[...] = sum(
+        mm(pick[:, 128 * dq:128 * dq + 128], errs[:, dq].reshape(256, 128), NT) for dq in range(6)
+    ).astype(bf16)
+    copies = [send(col3, col3_in.at[0], shifted(0, 1, 0)), send(col3, col3_in.at[1], shifted(0, -1, 0))]
 
     def second_half_grads():
         ends = [
@@ -503,8 +534,8 @@
         ones_rows = [jnp.ones((32, 128), bf16)]
         grad2 = None
         for dq in range(4):
-            cols = jnp.concatenate([cols2(0, dq, ones_rows), cols2(1, dq, ones_rows)], axis=1)
-            err = jnp.concatenate([errs[0, dq], errs[1, dq]], axis=1)
+            cols = jnp.concatenate([cols2(w, dq + 1, ones_rows) for w in (1, 2)], axis=1)
+            err = jnp.concatenate([errs[w, dq + 1] for w in (1, 2)], axis=1)
             piece = mm(err, cols, NT)
             grad2 = piece if grad2 is None else grad2 + piece
         for l in range(7):
@@ -569,14 +600,25 @@
             acc = acc + slots[n]
         return acc
 
-    feat_out, copies2 = halo(
-        errs, wide3, deep3, corner3, v3, col3, col3_in, fs, 64, True, second_half_grads,
-        lambda a: (a[0], sum_x(a[1])),
-    )
+    feat_out, copies2 = second_half_grads()
+    inner = mm(errs[...].reshape(1536, 128), t["shift2"][...])
+    arrive(copies)
+    rows = [kept(has_below, col3_in[0]), kept(has_above, col3_in[1])]
+    edge = mm(jnp.concatenate(rows, axis=0), t["put3"][...], TN)
+    for wp in range(4):
+        for dp in range(6):
+            number = wp * 6 + dp
+            for k in range(3):
+                piece = inner[number * 64:number * 64 + 64, 128 * k:128 * k + 128]
+                if k != 1:
+                    lane = dp * 256 + 64 * k
+                    piece = piece + edge[wp * 64:wp * 64 + 64, lane:lane + 128]
+                fs[number, (2 - k) * 64:(2 - k) * 64 + 64, :] = piece.astype(bf16)
+    copies2 = sum_x(copies2)
 
     for dq in range(4):
         def cols3(w):
-            taps = [fs[tile(w + 2 - i, dq + 2 - j)] for i in range(3) for j in range(3)]
+            taps = [fs[(w + 2 - i) * 6 + dq + 2 - j] for i in range(3) for j in range(3)]
             return jnp.concatenate(taps + [jnp.zeros((64, 128), bf16)], axis=0)
 
         cols = jnp.concatenate([cols3(0), cols3(1)], axis=1)
@@ -648,7 +690,7 @@
         volume, first_filters, first_bias.reshape(1, 32), second_filters, second_bias.reshape(1, 64),
         cotangent.transpose(1, 2, 3, 0).reshape(128, 64), jnp.asarray(PACKED),
     ]
-    sems = 78 + 4 + 3 * (NX - 1) + 3 * (GY - 1) + 2 * (NZ - 1)
+    sems = 62 + 4 + 3 * (NX - 1) + 3 * (GY - 1) + 2 * (NZ - 1)
     V = pltpu.VMEM
     results = (
         jax.ShapeDtypeStruct((128, 64), bf16),
@@ -666,10 +708,11 @@
             V((32, 128), bf16), V((2, 4, 16, 128), bf16), V((2, 16, 128), bf16), V((4, 16, 128), bf16),
             V((16, 128), bf16), V((2, 3, 3, 16, 128), bf16), V((64, 2, 16, 128), bf16), V((4, 8, 32, 256), f32),
             V((2, 8, 32, 128), bf16),
-            V((2, 4, 32, 128), bf16), V((2, 4, 32, 128), bf16), V((2, 2, 32, 128), bf16), V((4, 32, 128), bf16),
-            V((24, 32, 128), bf16), V((16, 128), bf16), V((2, 3, 3, 16, 128), bf16), V((24, 96, 128), bf16),
-            V((2, 4, 64, 128), bf16), V((2, 4, 64, 128), bf16), V((2, 2, 64, 128), bf16), V((4, 64, 128), bf16),
-            V((24, 64, 128), bf16), V((16, 128), bf16), V((2, 3, 3, 16, 128), bf16), V((24, 192, 128), bf16),
+            V((2, 128, 64), bf16), V((2, 32, 64), bf16), V((4, 32, 64), bf16),
+            V((2, 4, 32, 128), bf16), V((2, 2, 32, 128), bf16), V((2, 2, 4, 32, 128), bf16),
+            V((2, 2, 32, 128), bf16), V((4, 2, 32, 128), bf16), V((48, 32, 128), bf16),
+            V((16, 128), bf16), V((2, 3, 3, 16, 128), bf16), V((48, 96, 128), bf16),
+            V((4, 6, 64, 128), bf16), V((32, 256), bf16), V((2, 32, 256), bf16), V((24, 192, 128), bf16),
             V((32, 1792), bf16), V((2, 8, 32, 128), f32),
             V((512, 128), f32), V((256, 128), f32), V((256, 128), f32), V((NX - 1, n2, 128), f32),
             V((n2, 128), f32), V((GY - 1, n3, 128), f32), V((n3, 128), f32), V((NZ, n3, 128), f32),

time: 59.3 us -> 60.1 us (1.013)
  Pallas kernels: 58.6 us -> 59.4 us
    pallas_call x1, Pallas kernels: 56.8 us -> 57.6 us  [shards(): pl.pallas_call(functools.partial(kernel, (GX, GY, GZ, NX)), out_shape=res...]
where the time goes in v5:
time: 60.1 us; the launch traced here: 60 us
  Pallas kernels  59.4 us (99%)
  between operations  0.64 us (1%)
    pallas_call x1, Pallas kernels, shards(): pl.pallas_call(functools.partial(kernel, (GX, GY, GZ, NX)), out_shape=res...  57.6 us
    pallas_call x1, Pallas kernels, shards(): pl.pallas_call(hand_on, out_shape=results, in_specs=[pl.BlockSpec(memory_...  1.76 us

profile of v5, /device:TPU:1, one launch (start us, length us, event | category | flops | bytes accessed | tf_op | source)
XLA Modules:
  0.0 60.0 jit_solution(4731267855079616052)
XLA Ops:
  0.6 57.6 %shard_map.110 = (bf16[128,64]{1,0:T(8,128)(2,1)}, f32[32,108]{1,0:T(8,128)}, f32[1,32]{1,0:T(1,128)}, f32[64,864]{1,0:T(8,128)}, f32[1,64]{1,0:T(1,128)}) custom-call(bf16[4,4,16,128]{3,2,1,0:T(8,128)(2,1)} %refs_0_.1, f32[32,108]{1,0:T(8,128)} %refs_1_.1, f32[1,32]{1,0:T(1,128)} %bitcast.11, f32[64,864]{1,0:T(8,128)} %refs_3_.1, f32[1,64]{1,0:T(1,128)} %bitcast.12, ...), custom_call_target="tpu_custom_call" | custom-call | tf_op jit(solution)/shard_map/pallas_call | solution.py:702
  58.2 1.8 %shard_map.111 = (bf16[128,64]{1,0:T(8,128)(2,1)}, f32[32,108]{1,0:T(8,128)}, f32[1,32]{1,0:T(1,128)}, f32[64,864]{1,0:T(8,128)}, f32[1,64]{1,0:T(1,128)}) custom-call(bf16[128,64]{1,0:T(8,128)(2,1)} %get-tuple-element.15.refs_0_, f32[32,108]{1,0:T(8,128)} %get-tuple-element.16.refs_1_, f32[1,32]{1,0:T(1,128)} %get-tuple-element.17.refs_2_, ...), custom_call_target="tpu_custom_call" | custom-call | tf_op jit(solution)/shard_map/pallas_call | solution.py:732

commit v6 on v5

--- a/solution.py
+++ b/solution.py
@@ -213,8 +213,8 @@
         edges, wide_in, deep_in, corner_in, col1, col1_in, xs, pre1, summed,
         wide_t, deep_t, corner_t, pooled, packs, wide2, deep2, corner2, v2, col2, col2_in, ys,
         errs, col3, col3_in, fs, turned, perr,
-        grads, core_in, red1, x_in, red2, y_in, red3, z_in, total,
-        one, one_core, one_x, one_y, one_z, one_total, send_sems, recv_sems, vol, filt1, bias1, filt2, bias2, cot, packed, in_sems,
+        grads, core_in, red1, plane_in, z_in, total,
+        one, one_core, one_plane, one_z, one_total, send_sems, recv_sems, vol, filt1, bias1, filt2, bias2, cot, packed, in_sems,
         feat, step1, off1, step2, off2, out_sems,
     ) = refs[5:]
     near = (vol, filt1, bias1, filt2, bias2, cot, packed)
@@ -233,13 +233,12 @@
 
     sibling = (gx + 1 - 2 * core, gy, gz)
 
-    def x_peer(r):
-        p = lax.rem(xc + r, NX)
-        return p, (gx, gy, zl * NX + p)
-
-    def y_peer(r):
-        p = lax.rem(gy + r, GY)
-        return p, (gx, p, gz)
+    plane = xc * GY + gy
+    NP = NX * GY
+
+    def plane_peer(r):
+        p = lax.rem(plane + r, NP)
+        return p, (gx, lax.rem(p, GY), zl * NX + lax.div(p, GY))
 
     def z_peer(r):
         p = lax.rem(zc + r, NZ)
@@ -248,8 +247,7 @@
     square = [(dx, dz) for dx in (-1, 0, 1) for dz in (-1, 0, 1)]
     peers = [shifted(dx, 0, dz) for dx, dz in square if (dx, dz) != (0, 0)]
     peers += [shifted(dx, dy, dz) for dx, dz in square for dy in (-1, 1)]
-    peers += [x_peer(r)[1] for r in range(1, NX)]
-    peers += [y_peer(r)[1] for r in range(1, GY)]
+    peers += [plane_peer(r)[1] for r in range(1, NP)]
     peers += [z_peer(r) for r in range(1, NZ)]
     barrier = pltpu.get_barrier_semaphore()
     for peer in peers:
@@ -546,43 +544,29 @@
     def part(ref, index, size):
         return ref.at[pl.ds(pl.multiple_of(index * size, size), size)]
 
-    n1, n2, n3 = 256, 256 // NX, 256 // NX // GY
+    n1, n3 = 256, 256 // NP
 
     def sum_core(copy):
         copy.wait_recv()
         red1[...] = part(grads, core, n1)[...] + core_in[...]
-        return [send(part(red1, x_peer(r)[0], n2), x_in.at[r - 1], x_peer(r)[1]) for r in range(1, NX)]
-
-    def sum_x(copies):
+        return [send(part(red1, plane_peer(r)[0], n3), plane_in.at[r - 1], plane_peer(r)[1]) for r in range(1, NP)]
+
+    def sum_plane(copies):
         arrive(copies)
-        acc = part(red1, xc, n2)[...]
-        for r in range(1, NX):
-            acc = acc + x_in[r - 1]
-        red2[...] = acc
-        return [send(part(red2, y_peer(r)[0], n3), y_in.at[r - 1], y_peer(r)[1]) for r in range(1, GY)]
-
-    def sum_y(copies):
-        arrive(copies)
-        acc = part(red2, gy, n3)[...]
-        for r in range(1, GY):
-            acc = acc + y_in[r - 1]
-        red3[...] = acc
+        acc = part(red1, plane, n3)[...]
+        for r in range(1, NP):
+            acc = acc + plane_in[r - 1]
         z_in[zc] = acc
-        return [send(red3, z_in.at[zc], z_peer(r)) for r in range(1, NZ)]
+        return [send(z_in.at[zc], z_in.at[zc], z_peer(r)) for r in range(1, NZ)]
 
     def sum_z(copies):
         arrive(copies)
         acc = z_in[0]
         for r in range(1, NZ):
             acc = acc + z_in[r]
-        mine = part(total, (core * NX + xc) * GY + gy, n3)
+        mine = part(total, core * NP + plane, n3)
         mine[...] = acc
-        return [send(mine, mine, y_peer(r)[1]) for r in range(1, GY)]
-
-    def gather_x(copies):
-        arrive(copies)
-        mine = part(total, core * NX + xc, n2)
-        return [send(mine, mine, x_peer(r)[1]) for r in range(1, NX)]
+        return [send(mine, mine, plane_peer(r)[1]) for r in range(1, NP)]
 
     def gather_core(copies):
         arrive(copies)
@@ -614,7 +598,6 @@
                     lane = dp * 256 + 64 * k
                     piece = piece + edge[wp * 64:wp * 64 + 64, lane:lane + 128]
                 fs[number, (2 - k) * 64:(2 - k) * 64 + 64, :] = piece.astype(bf16)
-    copies2 = sum_x(copies2)
 
     for dq in range(4):
         def cols3(w):
@@ -628,8 +611,6 @@
             perr[w, dq] = both[32 * w:32 * w + 32, :128]
             perr[w, dq + 4] = both[32 * w:32 * w + 32, 128:]
 
-    copies2 = sum_y(copies2)
-
     def backward1(pd, acc):
         for w in range(4):
             here = perr[w // 2, pd]
@@ -640,21 +621,22 @@
     grad1 = lax.fori_loop(0, 8, backward1, jnp.zeros((32, 144), f32))
     one[...] = sum(mm(piece, t["narrow"][...]) for piece in split3(grad1))
     copies1 = send(part(one, 1 - core, 16), one_core, sibling)
+    copies2 = sum_plane(copies2)
     copies1.wait_recv()
-    copies1 = everyone(part(one, core, 16)[...] + one_core[...], one_x, xc, [x_peer(r)[1] for r in range(1, NX)])
+    copies1 = everyone(
+        part(one, core, 16)[...] + one_core[...], one_plane, plane, [plane_peer(r)[1] for r in range(1, NP)]
+    )
     copies2 = sum_z(copies2)
-    copies1 = everyone(summed_slots(copies1, one_x), one_y, gy, [y_peer(r)[1] for r in range(1, GY)])
-    copies2 = gather_x(copies2)
-    copies1 = everyone(summed_slots(copies1, one_y), one_z, zc, [z_peer(r) for r in range(1, NZ)])
+    copies1 = everyone(summed_slots(copies1, one_plane), one_z, zc, [z_peer(r) for r in range(1, NZ)])
     copy2 = gather_core(copies2)
+    mine = part(one_total, core, 16)
+    mine[...] = summed_slots(copies1, one_z)
+    copy1 = send(mine, mine, sibling)
     copy2.wait_recv()
     sums2 = jnp.concatenate([total[l * 64:l * 64 + 64] for l in range(7)], axis=1)
     step2[...] = filt2[...] - learn_rate * sums2[:, :864]
     off2[...] = bias2[...] - learn_rate * column_to_row(sums2[:, 864:865])
     outs = [put_out(3), put_out(4)]
-    mine = part(one_total, core, 16)
-    mine[...] = summed_slots(copies1, one_z)
-    copy1 = send(mine, mine, sibling)
     copy1.wait_recv()
     sums1 = one_total[...]
     step1[...] = filt1[...] - learn_rate * sums1[:, :108]
@@ -685,12 +667,13 @@
     GX, GY, GZ = lax.axis_size("gx"), lax.axis_size("gy"), lax.axis_size("gz")
     NX = 4 if GZ >= 8 else 2
     NZ = (GX // 2) * (GZ // NX)
-    n2, n3 = 256 // NX, 256 // NX // GY
+    NP = NX * GY
+    n3 = 256 // NP
     operands = [
         volume, first_filters, first_bias.reshape(1, 32), second_filters, second_bias.reshape(1, 64),
         cotangent.transpose(1, 2, 3, 0).reshape(128, 64), jnp.asarray(PACKED),
     ]
-    sems = 62 + 4 + 3 * (NX - 1) + 3 * (GY - 1) + 2 * (NZ - 1)
+    sems = 62 + 4 + 3 * (NP - 1) + 2 * (NZ - 1)
     V = pltpu.VMEM
     results = (
         jax.ShapeDtypeStruct((128, 64), bf16),
@@ -714,10 +697,10 @@
             V((16, 128), bf16), V((2, 3, 3, 16, 128), bf16), V((48, 96, 128), bf16),
             V((4, 6, 64, 128), bf16), V((32, 256), bf16), V((2, 32, 256), bf16), V((24, 192, 128), bf16),
             V((32, 1792), bf16), V((2, 8, 32, 128), f32),
-            V((512, 128), f32), V((256, 128), f32), V((256, 128), f32), V((NX - 1, n2, 128), f32),
-            V((n2, 128), f32), V((GY - 1, n3, 128), f32), V((n3, 128), f32), V((NZ, n3, 128), f32),
+            V((512, 128), f32), V((256, 128), f32), V((256, 128), f32), V((NP - 1, n3, 128), f32),
+            V((NZ, n3, 128), f32),
             V((512, 128), f32),
-            V((32, 128), f32), V((16, 128), f32), V((NX, 16, 128), f32), V((GY, 16, 128), f32),
+            V((32, 128), f32), V((16, 128), f32), V((NP, 16, 128), f32),
             V((NZ, 16, 128), f32), V((32, 128), f32),
             pltpu.SemaphoreType.DMA((sems,)), pltpu.SemaphoreType.DMA((sems,)),
         ] + [V(a.shape, a.dtype) for a in operands] + [

time: 60.1 us -> 55.5 us (0.923)
  Pallas kernels: 59.4 us -> 54.7 us
    pallas_call x1, Pallas kernels: 57.6 us -> 53 us  [shards(): pl.pallas_call(functools.partial(kernel, (GX, GY, GZ, NX)), out_shape=res...]
where the time goes in v6:
time: 55.5 us; the launch traced here: 55.4 us
  Pallas kernels  54.7 us (99%)
  between operations  0.64 us (1%)
    pallas_call x1, Pallas kernels, shards(): pl.pallas_call(functools.partial(kernel, (GX, GY, GZ, NX)), out_shape=res...  53 us
    pallas_call x1, Pallas kernels, shards(): pl.pallas_call(hand_on, out_shape=results, in_specs=[pl.BlockSpec(memory_...  1.76 us

profile of v6, /device:TPU:1, one launch (start us, length us, event | category | flops | bytes accessed | tf_op | source)
XLA Modules:
  0.0 55.4 jit_solution(10587619138129733092)
XLA Ops:
  0.6 53.0 %shard_map.110 = (bf16[128,64]{1,0:T(8,128)(2,1)}, f32[32,108]{1,0:T(8,128)}, f32[1,32]{1,0:T(1,128)}, f32[64,864]{1,0:T(8,128)}, f32[1,64]{1,0:T(1,128)}) custom-call(bf16[4,4,16,128]{3,2,1,0:T(8,128)(2,1)} %refs_0_.1, f32[32,108]{1,0:T(8,128)} %refs_1_.1, f32[1,32]{1,0:T(1,128)} %bitcast.11, f32[64,864]{1,0:T(8,128)} %refs_3_.1, f32[1,64]{1,0:T(1,128)} %bitcast.12, ...), custom_call_target="tpu_custom_call" | custom-call | tf_op jit(solution)/shard_map/pallas_call | solution.py:685
  53.6 1.8 %shard_map.111 = (bf16[128,64]{1,0:T(8,128)(2,1)}, f32[32,108]{1,0:T(8,128)}, f32[1,32]{1,0:T(1,128)}, f32[64,864]{1,0:T(8,128)}, f32[1,64]{1,0:T(1,128)}) custom-call(bf16[128,64]{1,0:T(8,128)(2,1)} %get-tuple-element.15.refs_0_, f32[32,108]{1,0:T(8,128)} %get-tuple-element.16.refs_1_, f32[1,32]{1,0:T(1,128)} %get-tuple-element.17.refs_2_, ...), custom_call_target="tpu_custom_call" | custom-call | tf_op jit(solution)/shard_map/pallas_call | solution.py:715

commit v7 on v6

--- a/solution.py
+++ b/solution.py
@@ -210,7 +210,7 @@
     refs = refs[7:]
     far_out = refs[:5]
     (
-        edges, wide_in, deep_in, corner_in, col1, col1_in, xs, pre1, summed,
+        edges, wide_in, deep_in, corner_in, col1, col1_in, xs, pre1,
         wide_t, deep_t, corner_t, pooled, packs, wide2, deep2, corner2, v2, col2, col2_in, ys,
         errs, col3, col3_in, fs, turned, perr,
         grads, core_in, red1, plane_in, z_in, total,
@@ -236,19 +236,27 @@
     plane = xc * GY + gy
     NP = NX * GY
 
-    def plane_peer(r):
-        p = lax.rem(plane + r, NP)
-        return p, (gx, lax.rem(p, GY), zl * NX + lax.div(p, GY))
+    def ring_gap(n, r):
+        return min(r, n - r)
+
+    plane_steps = [(rx, ry) for rx in range(NX) for ry in range(GY) if rx or ry]
+    plane_steps.sort(key=lambda step: -ring_gap(NX, step[0]) - ring_gap(GY, step[1]))
+    z_steps = sorted(range(1, NZ), key=lambda r: -ring_gap(NZ, r))
+
+    def plane_peer(step):
+        px, py = lax.rem(xc + step[0], NX), lax.rem(gy + step[1], GY)
+        return px * GY + py, (gx, py, zl * NX + px)
 
     def z_peer(r):
         p = lax.rem(zc + r, NZ)
         return (2 * lax.div(p, ZL) + core, gy, lax.rem(p, ZL) * NX + xc)
 
-    square = [(dx, dz) for dx in (-1, 0, 1) for dz in (-1, 0, 1)]
-    peers = [shifted(dx, 0, dz) for dx, dz in square if (dx, dz) != (0, 0)]
-    peers += [shifted(dx, dy, dz) for dx, dz in square for dy in (-1, 1)]
-    peers += [plane_peer(r)[1] for r in range(1, NP)]
-    peers += [z_peer(r) for r in range(1, NZ)]
+    square = [(dx, dz) for dx in (-1, 1, 0) for dz in (-1, 1, 0)]
+    square.sort(key=lambda step: -abs(step[0]) - abs(step[1]))
+    peers = [shifted(dx, dy, dz) for dx, dz in square for dy in (-1, 1)]
+    peers += [shifted(dx, 0, dz) for dx, dz in square if (dx, dz) != (0, 0)]
+    peers += [plane_peer(step)[1] for step in plane_steps]
+    peers += [z_peer(r) for r in z_steps]
     barrier = pltpu.get_barrier_semaphore()
     for peer in peers:
         pl.semaphore_signal(barrier, inc=1, device_id=peer, device_id_type=MESH)
@@ -266,6 +274,10 @@
         copy.start()
         started.append(copy)
         return copy
+
+    def drain(keep):
+        while len(started) > keep:
+            started.pop(0).wait_send()
 
     def put_out(n):
         copy = pltpu.make_async_copy((feat, step1, off1, step2, off2)[n], far_out[n], out_sems.at[n])
@@ -413,26 +425,6 @@
             [jnp.concatenate(one, axis=0), jnp.concatenate(two, axis=0)], axis=1
         )
 
-    def forward1(pd, carry):
-        for pw in range(2):
-            part = None
-            for w in (2 * pw, 2 * pw + 1):
-                pre = mm(wide_first, cols1(w, pd)) + bias1_col
-                pre1[w, pd] = pre
-                act = leaky(pre)
-                act = act[:, :128] + act[:, 128:]
-                part = act if part is None else part + act
-            part = (part + pltpu.roll(part, 127, axis=1)) * 0.125
-            summed[pw, pd] = part.astype(bf16)
-        return carry
-
-    lax.fori_loop(0, 8, forward1, 0)
-    pooled_val = (
-        mm(summed[:, 0:4].reshape(256, 128), t["even"][0:128])
-        + mm(summed[:, 4:8].reshape(256, 128), t["even"][128:256])
-    ).astype(bf16)
-    pooled[...] = pooled_val.reshape(2, 4, 32, 128)
-
     def turned_half(a):
         return pltpu.roll(a.astype(f32), 64, axis=1)
 
@@ -441,12 +433,35 @@
     def halves(a, b):
         return jnp.where(low, a.astype(f32), b.astype(f32)).astype(bf16)
 
-    for w in range(2):
-        packs[0, w] = halves(turned_half(pooled[w, 2]), pooled[w, 3])
-        packs[1, w] = halves(pooled[w, 0], turned_half(pooled[w, 1]))
-    copies = send_ring(
-        lambda a: pooled, wide2, lambda b: packs.at[b], deep2, lambda a, b: packs.at[b], corner2
-    )
+    copies = []
+    for dq in range(4):
+        sums = [[None, None], [None, None]]
+        for half in range(2):
+            pd = dq + 4 * half
+            for pw in range(2):
+                both = None
+                for w in (2 * pw, 2 * pw + 1):
+                    pre = mm(wide_first, cols1(w, pd)) + bias1_col
+                    pre1[w, pd] = pre
+                    act = leaky(pre)
+                    act = act[:, :128] + act[:, 128:]
+                    both = act if both is None else both + act
+                sums[pw][half] = ((both + pltpu.roll(both, 127, axis=1)) * 0.125).astype(bf16)
+        lanes = [jnp.concatenate([sums[0][half], sums[1][half]], axis=0) for half in range(2)]
+        value = (mm(lanes[0], t["even"][0:128]) + mm(lanes[1], t["even"][128:256])).astype(bf16)
+        pooled[:, dq] = value.reshape(2, 32, 128)
+        for a in range(2):
+            copies.append(send(pooled.at[:, dq], wide2.at[a, :, dq], shifted(1 - 2 * a, 0, 0)))
+        if dq % 2:
+            b = 0 if dq == 3 else 1
+            for w in range(2):
+                if b == 0:
+                    packs[0, w] = halves(turned_half(pooled[w, 2]), pooled[w, 3])
+                else:
+                    packs[1, w] = halves(pooled[w, 0], turned_half(pooled[w, 1]))
+            copies.append(send(packs.at[b], deep2.at[b], shifted(0, 0, 1 - 2 * b)))
+            for a in range(2):
+                copies.append(send(packs.at[b], corner2.at[a * 2 + b], shifted(1 - 2 * a, 0, 1 - 2 * b)))
     pick = t["pick2"][...]
     ends = sum(
         mm(pick[:, 128 * dq:128 * dq + 128], pooled[:, dq].reshape(64, 128), NT) for dq in range(4)
@@ -549,7 +564,11 @@
     def sum_core(copy):
         copy.wait_recv()
         red1[...] = part(grads, core, n1)[...] + core_in[...]
-        return [send(part(red1, plane_peer(r)[0], n3), plane_in.at[r - 1], plane_peer(r)[1]) for r in range(1, NP)]
+        copies = []
+        for n, step in enumerate(plane_steps):
+            p, device = plane_peer(step)
+            copies.append(send(part(red1, p, n3), plane_in.at[n], device))
+        return copies
 
     def sum_plane(copies):
         arrive(copies)
@@ -557,7 +576,7 @@
         for r in range(1, NP):
             acc = acc + plane_in[r - 1]
         z_in[zc] = acc
-        return [send(z_in.at[zc], z_in.at[zc], z_peer(r)) for r in range(1, NZ)]
+        return [send(z_in.at[zc], z_in.at[zc], z_peer(r)) for r in z_steps]
 
     def sum_z(copies):
         arrive(copies)
@@ -566,7 +585,7 @@
             acc = acc + z_in[r]
         mine = part(total, core * NP + plane, n3)
         mine[...] = acc
-        return [send(mine, mine, plane_peer(r)[1]) for r in range(1, NP)]
+        return [send(mine, mine, plane_peer(step)[1]) for step in plane_steps]
 
     def gather_core(copies):
         arrive(copies)
@@ -611,24 +630,26 @@
             perr[w, dq] = both[32 * w:32 * w + 32, :128]
             perr[w, dq + 4] = both[32 * w:32 * w + 32, 128:]
 
-    def backward1(pd, acc):
+    grad1 = None
+    for pd in range(8):
         for w in range(4):
             here = perr[w // 2, pd]
             err = (jnp.concatenate([here, here], axis=1) * slope(pre1[w, pd])).astype(bf16)
-            acc = acc + mm(err, cols1(w, pd), NT)
-        return acc
-
-    grad1 = lax.fori_loop(0, 8, backward1, jnp.zeros((32, 144), f32))
+            piece = mm(err, cols1(w, pd), NT)
+            grad1 = piece if grad1 is None else grad1 + piece
     one[...] = sum(mm(piece, t["narrow"][...]) for piece in split3(grad1))
     copies1 = send(part(one, 1 - core, 16), one_core, sibling)
     copies2 = sum_plane(copies2)
+    drain(NP + NZ)
     copies1.wait_recv()
     copies1 = everyone(
-        part(one, core, 16)[...] + one_core[...], one_plane, plane, [plane_peer(r)[1] for r in range(1, NP)]
-    )
+        part(one, core, 16)[...] + one_core[...], one_plane, plane, [plane_peer(step)[1] for step in plane_steps]
+    )
+    drain(NP)
     copies2 = sum_z(copies2)
-    copies1 = everyone(summed_slots(copies1, one_plane), one_z, zc, [z_peer(r) for r in range(1, NZ)])
+    copies1 = everyone(summed_slots(copies1, one_plane), one_z, zc, [z_peer(r) for r in z_steps])
     copy2 = gather_core(copies2)
+    drain(1)
     mine = part(one_total, core, 16)
     mine[...] = summed_slots(copies1, one_z)
     copy1 = send(mine, mine, sibling)
@@ -643,8 +664,7 @@
     off1[...] = bias1[...] - learn_rate * column_to_row(sums1[:, 108:109])
     outs += [put_out(1), put_out(2)]
 
-    for copy in started:
-        copy.wait_send()
+    drain(0)
     feat_out.wait()
     for out in outs:
         out.wait()
@@ -673,7 +693,7 @@
         volume, first_filters, first_bias.reshape(1, 32), second_filters, second_bias.reshape(1, 64),
         cotangent.transpose(1, 2, 3, 0).reshape(128, 64), jnp.asarray(PACKED),
     ]
-    sems = 62 + 4 + 3 * (NP - 1) + 2 * (NZ - 1)
+    sems = 68 + 4 + 3 * (NP - 1) + 2 * (NZ - 1)
     V = pltpu.VMEM
     results = (
         jax.ShapeDtypeStruct((128, 64), bf16),
@@ -690,7 +710,6 @@
         scratch_shapes=[
             V((32, 128), bf16), V((2, 4, 16, 128), bf16), V((2, 16, 128), bf16), V((4, 16, 128), bf16),
             V((16, 128), bf16), V((2, 3, 3, 16, 128), bf16), V((64, 2, 16, 128), bf16), V((4, 8, 32, 256), f32),
-            V((2, 8, 32, 128), bf16),
             V((2, 128, 64), bf16), V((2, 32, 64), bf16), V((4, 32, 64), bf16),
             V((2, 4, 32, 128), bf16), V((2, 2, 32, 128), bf16), V((2, 2, 4, 32, 128), bf16),
             V((2, 2, 32, 128), bf16), V((4, 2, 32, 128), bf16), V((48, 32, 128), bf16),

time: 55.5 us -> 52.4 us (0.944)
  Pallas kernels: 54.7 us -> 51.7 us
    pallas_call x1, Pallas kernels: 53 us -> 49.9 us  [shards(): pl.pallas_call(functools.partial(kernel, (GX, GY, GZ, NX)), out_shape=res...]
where the time goes in v7:
time: 52.4 us; the launch traced here: 52.3 us
  Pallas kernels  51.7 us (99%)
  between operations  0.64 us (1%)
    pallas_call x1, Pallas kernels, shards(): pl.pallas_call(functools.partial(kernel, (GX, GY, GZ, NX)), out_shape=res...  49.9 us
    pallas_call x1, Pallas kernels, shards(): pl.pallas_call(hand_on, out_shape=results, in_specs=[pl.BlockSpec(memory_...  1.76 us

profile of v7, /device:TPU:1, one launch (start us, length us, event | category | flops | bytes accessed | tf_op | source)
XLA Modules:
  0.0 52.3 jit_solution(571145456343123021)
XLA Ops:
  0.6 49.9 %shard_map.110 = (bf16[128,64]{1,0:T(8,128)(2,1)}, f32[32,108]{1,0:T(8,128)}, f32[1,32]{1,0:T(1,128)}, f32[64,864]{1,0:T(8,128)}, f32[1,64]{1,0:T(1,128)}) custom-call(bf16[4,4,16,128]{3,2,1,0:T(8,128)(2,1)} %refs_0_.1, f32[32,108]{1,0:T(8,128)} %refs_1_.1, f32[1,32]{1,0:T(1,128)} %bitcast.11, f32[64,864]{1,0:T(8,128)} %refs_3_.1, f32[1,64]{1,0:T(1,128)} %bitcast.12, ...), custom_call_target="tpu_custom_call" | custom-call | tf_op jit(solution)/shard_map/pallas_call | solution.py:705
  50.6 1.8 %shard_map.111 = (bf16[128,64]{1,0:T(8,128)(2,1)}, f32[32,108]{1,0:T(8,128)}, f32[1,32]{1,0:T(1,128)}, f32[64,864]{1,0:T(8,128)}, f32[1,64]{1,0:T(1,128)}) custom-call(bf16[128,64]{1,0:T(8,128)(2,1)} %get-tuple-element.15.refs_0_, f32[32,108]{1,0:T(8,128)} %get-tuple-element.16.refs_1_, f32[1,32]{1,0:T(1,128)} %get-tuple-element.17.refs_2_, ...), custom_call_target="tpu_custom_call" | custom-call | tf_op jit(solution)/shard_map/pallas_call | solution.py:734

commit v8 on v7

--- a/solution.py
+++ b/solution.py
@@ -109,10 +109,11 @@
     for dc in range(4):
         for hc in range(32):
             collect[(dc % 2) * 128 + dc * 32 + hc, (dc // 2) * 64 + 2 * hc] = 1
-    widen = np.zeros((108, 144))
+    widen = np.zeros((108, 1536))
     narrow = np.zeros((144, 128))
     for q in range(108):
-        widen[q, (q // 12) * 16 + q % 12] = 1
+        for w in range(4):
+            widen[q, w * 384 + w * 48 + (q // 12) * 16 + q % 12] = 1
         narrow[(q // 12) * 16 + q % 12, q] = 1
     narrow[12, 108] = 1
     ident = np.zeros((64, 256))
@@ -208,15 +209,15 @@
     NZ = ZH * ZL
     far = refs[:7]
     refs = refs[7:]
-    far_out = refs[:5]
+    feat_out, one_out, total_out = refs[:3]
     (
         edges, wide_in, deep_in, corner_in, col1, col1_in, xs, pre1,
         wide_t, deep_t, corner_t, pooled, packs, wide2, deep2, corner2, v2, col2, col2_in, ys,
         errs, col3, col3_in, fs, turned, perr,
         grads, core_in, red1, plane_in, z_in, total,
-        one, one_core, one_plane, one_z, one_total, send_sems, recv_sems, vol, filt1, bias1, filt2, bias2, cot, packed, in_sems,
-        feat, step1, off1, step2, off2, out_sems,
-    ) = refs[5:]
+        one, one_core, one_plane, one_z, one_half, send_sems, recv_sems, vol, filt1, bias1, filt2, bias2, cot, packed, in_sems,
+        feat, base1, base2, out_sems,
+    ) = refs[3:]
     near = (vol, filt1, bias1, filt2, bias2, cot, packed)
     fetches = [pltpu.make_async_copy(a, b, in_sems.at[n]) for n, (a, b) in enumerate(zip(far, near))]
     for fetch in fetches:
@@ -279,10 +280,12 @@
         while len(started) > keep:
             started.pop(0).wait_send()
 
-    def put_out(n):
-        copy = pltpu.make_async_copy((feat, step1, off1, step2, off2)[n], far_out[n], out_sems.at[n])
+    outs = []
+
+    def put_out(src, dst):
+        copy = pltpu.make_async_copy(src, dst, out_sems.at[len(outs)])
         copy.start()
-        return copy
+        outs.append(copy)
 
     def arrive(copies):
         for copy in copies:
@@ -359,8 +362,17 @@
     for fetch in fetches[1:]:
         fetch.wait()
     first_half = filt1[...].astype(bf16)
+    base1[...] = jnp.concatenate([filt1[...], row_to_column(bias1[...]), jnp.zeros((32, 19), f32)], axis=1)
+    for l in range(6):
+        base2[64 * l:64 * l + 64] = filt2[:, 128 * l:128 * l + 128]
+    base2[384:448] = jnp.concatenate(
+        [filt2[:, 768:864], jnp.broadcast_to(row_to_column(bias2[...]), (64, 32))], axis=1
+    )
+    base2[448:512] = jnp.zeros((64, 128), f32)
     wide_first = mm(first_half, t["widen"][...]).astype(bf16)
+    wide_first = jnp.concatenate([wide_first[:, 384 * w:384 * w + 288] for w in range(4)], axis=0)
     bias1_col = row_to_column(bias1[...])
+    bias1_col = jnp.concatenate([bias1_col] * 4, axis=0)
     bias2_col = row_to_column(bias2[...])
     second_half = filt2[...].astype(bf16)
 
@@ -370,11 +382,17 @@
     )
 
     turn = mm(second_half, t["ident"][...], TN).astype(bf16)
-    for m in range(13):
-        low = turn[64 * m:64 * m + 32, :128].astype(f32)
-        high = turn[64 * m + 32:64 * m + 64, 128:].astype(f32)
-        turned[:, 128 * m:128 * m + 128] = (low + high).astype(bf16)
-    turned[:, 1664:1792] = turn[832:864, :128]
+    for w in range(2):
+        for m in range(18):
+            pair = []
+            for high in range(2):
+                wp, rest = divmod(2 * m + high, 9)
+                i = w + 2 - wp
+                if 0 <= i <= 2:
+                    tap = 9 * i + rest
+                    pair.append(turn[32 * tap:32 * tap + 32, 128 * high:128 * high + 128].astype(f32))
+            value = sum(pair) if pair else jnp.zeros((32, 128), f32)
+            turned[32 * w:32 * w + 32, 128 * m:128 * m + 128] = value.astype(bf16)
 
     arrive(copies)
     pieces = [block]
@@ -415,15 +433,12 @@
     xs[:, 0] = even_tile.astype(bf16)
     xs[:, 1] = odd_tile.astype(bf16)
 
-    def cols1(w, half_d):
-        def at(i, dp, parity):
-            return xs[(w + i) * 9 + dp, parity]
-
-        one = [at(i, half_d + j // 2, j % 2) for i in range(3) for j in range(3)]
-        two = [at(i, half_d + (j + 1) // 2, (j + 1) % 2) for i in range(3) for j in range(3)]
-        return jnp.concatenate(
-            [jnp.concatenate(one, axis=0), jnp.concatenate(two, axis=0)], axis=1
-        )
+    def cols1(half_d):
+        sides = []
+        for e in range(2):
+            tiles = [xs[wp * 9 + half_d + (j + e) // 2, (j + e) % 2] for wp in range(6) for j in range(3)]
+            sides.append(jnp.concatenate(tiles, axis=0))
+        return jnp.concatenate(sides, axis=1)
 
     def turned_half(a):
         return pltpu.roll(a.astype(f32), 64, axis=1)
@@ -438,14 +453,12 @@
         sums = [[None, None], [None, None]]
         for half in range(2):
             pd = dq + 4 * half
+            pre = mm(wide_first, cols1(pd)) + bias1_col
+            pre1[pd] = pre
+            act = leaky(pre)
+            act = act[:, :128] + act[:, 128:]
             for pw in range(2):
-                both = None
-                for w in (2 * pw, 2 * pw + 1):
-                    pre = mm(wide_first, cols1(w, pd)) + bias1_col
-                    pre1[w, pd] = pre
-                    act = leaky(pre)
-                    act = act[:, :128] + act[:, 128:]
-                    both = act if both is None else both + act
+                both = act[64 * pw:64 * pw + 32] + act[64 * pw + 32:64 * pw + 64]
                 sums[pw][half] = ((both + pltpu.roll(both, 127, axis=1)) * 0.125).astype(bf16)
         lanes = [jnp.concatenate([sums[0][half], sums[1][half]], axis=0) for half in range(2)]
         value = (mm(lanes[0], t["even"][0:128]) + mm(lanes[1], t["even"][128:256])).astype(bf16)
@@ -520,24 +533,23 @@
         return jnp.concatenate(taps + extra, axis=0)
 
     feat_sum = [None, None]
-    for dq in range(6):
-        kind = {0: 2, 5: 3}.get(dq, (dq - 1) // 2)
-        for pair in ((1, 2), (0, 3)):
-            cols = jnp.concatenate([cols2(w, dq, []) for w in pair], axis=1)
-            pre = mm(second_half, cols) + bias2_col
-            if pair == (1, 2) and 0 < dq < 5:
-                act = leaky(pre)
-                act = act[:, :128] + act[:, 128:]
-                feat_sum[kind] = act if feat_sum[kind] is None else feat_sum[kind] + act
-            for n, w in enumerate(pair):
-                here = spread_cot[(w + 1) // 2][:, 128 * kind:128 * kind + 128]
-                errs[w, dq] = (here * slope(pre[:, 128 * n:128 * n + 128])).astype(bf16)
-
-    pick = t["pick3"][...]
-    col3[...] = sum(
-        mm(pick[:, 128 * dq:128 * dq + 128], errs[:, dq].reshape(256, 128), NT) for dq in range(6)
-    ).astype(bf16)
-    copies = [send(col3, col3_in.at[0], shifted(0, 1, 0)), send(col3, col3_in.at[1], shifted(0, -1, 0))]
+
+    def errors(dqs, pairs):
+        for dq in dqs:
+            kind = {0: 2, 5: 3}.get(dq, (dq - 1) // 2)
+            for pair in pairs:
+                errors_of(dq, kind, pair)
+
+    def errors_of(dq, kind, pair):
+        cols = jnp.concatenate([cols2(w, dq, []) for w in pair], axis=1)
+        pre = mm(second_half, cols) + bias2_col
+        if pair == (1, 2) and 0 < dq < 5:
+            act = leaky(pre)
+            act = act[:, :128] + act[:, 128:]
+            feat_sum[kind] = act if feat_sum[kind] is None else feat_sum[kind] + act
+        for n, w in enumerate(pair):
+            here = spread_cot[(w + 1) // 2][:, 128 * kind:128 * kind + 128]
+            errs[w, dq] = (here * slope(pre[:, 128 * n:128 * n + 128])).astype(bf16)
 
     def second_half_grads():
         ends = [
@@ -554,7 +566,8 @@
         for l in range(7):
             grads[l * 64:l * 64 + 64] = grad2[:, 128 * l:128 * l + 128]
         grads[448:512] = jnp.zeros((64, 128), f32)
-        return put_out(0), sum_core(send(part(grads, 1 - core, n1), core_in, sibling))
+        put_out(feat, feat_out)
+        return send(part(grads, 1 - core, n1), core_in, sibling)
 
     def part(ref, index, size):
         return ref.at[pl.ds(pl.multiple_of(index * size, size), size)]
@@ -584,13 +597,15 @@
         for r in range(1, NZ):
             acc = acc + z_in[r]
         mine = part(total, core * NP + plane, n3)
-        mine[...] = acc
+        mine[...] = part(base2, core * NP + plane, n3)[...] - learn_rate * acc
         return [send(mine, mine, plane_peer(step)[1]) for step in plane_steps]
 
     def gather_core(copies):
         arrive(copies)
-        mine = part(total, core, n1)
-        return send(mine, mine, sibling)
+        mine, far = part(total, core, n1), part(total_out, core, n1)
+        copy = send(mine, far, sibling)
+        put_out(mine, far)
+        return copy
 
     def everyone(value, slots, index, devices):
         slots[index] = value
@@ -603,7 +618,14 @@
             acc = acc + slots[n]
         return acc
 
-    feat_out, copies2 = second_half_grads()
+    errors(range(0, 6), [(1, 2), (0, 3)])
+    pick = t["pick3"][...]
+    col3[...] = sum(
+        mm(pick[:, 128 * dq:128 * dq + 128], errs[:, dq].reshape(256, 128), NT) for dq in range(6)
+    ).astype(bf16)
+    copies = [send(col3, col3_in.at[0], shifted(0, 1, 0)), send(col3, col3_in.at[1], shifted(0, -1, 0))]
+
+    copies2 = sum_core(second_half_grads())
     inner = mm(errs[...].reshape(1536, 128), t["shift2"][...])
     arrive(copies)
     rows = [kept(has_below, col3_in[0]), kept(has_above, col3_in[1])]
@@ -618,25 +640,25 @@
                     piece = piece + edge[wp * 64:wp * 64 + 64, lane:lane + 128]
                 fs[number, (2 - k) * 64:(2 - k) * 64 + 64, :] = piece.astype(bf16)
 
-    for dq in range(4):
-        def cols3(w):
-            taps = [fs[(w + 2 - i) * 6 + dq + 2 - j] for i in range(3) for j in range(3)]
-            return jnp.concatenate(taps + [jnp.zeros((64, 128), bf16)], axis=0)
-
-        cols = jnp.concatenate([cols3(0), cols3(1)], axis=1)
-        pe = mm(turned[...], cols).astype(bf16)
+    def cols3(dq):
+        return jnp.concatenate([fs[wp * 6 + dq + 2 - j] for wp in range(4) for j in range(3)], axis=0)
+
+    for dq in (0, 2):
+        pe = mm(turned[...], jnp.concatenate([cols3(dq), cols3(dq + 1)], axis=1)).astype(bf16)
         both = mm(jnp.concatenate([pe[:, :128], pe[:, 128:]], axis=0), t["twice"][...]) * 0.125
-        for w in range(2):
-            perr[w, dq] = both[32 * w:32 * w + 32, :128]
-            perr[w, dq + 4] = both[32 * w:32 * w + 32, 128:]
+        for n in range(2):
+            for w in range(2):
+                rows = both[64 * n + 32 * w:64 * n + 32 * w + 32]
+                perr[w, dq + n] = rows[:, :128]
+                perr[w, dq + n + 4] = rows[:, 128:]
 
     grad1 = None
     for pd in range(8):
-        for w in range(4):
-            here = perr[w // 2, pd]
-            err = (jnp.concatenate([here, here], axis=1) * slope(pre1[w, pd])).astype(bf16)
-            piece = mm(err, cols1(w, pd), NT)
-            grad1 = piece if grad1 is None else grad1 + piece
+        here = jnp.concatenate([perr[w // 2, pd] for w in range(4)], axis=0)
+        err = (jnp.concatenate([here, here], axis=1) * slope(pre1[pd])).astype(bf16)
+        piece = mm(err, cols1(pd), NT)
+        grad1 = piece if grad1 is None else grad1 + piece
+    grad1 = sum(grad1[32 * w:32 * w + 32, 48 * w:48 * w + 144] for w in range(4))
     one[...] = sum(mm(piece, t["narrow"][...]) for piece in split3(grad1))
     copies1 = send(part(one, 1 - core, 16), one_core, sibling)
     copies2 = sum_plane(copies2)
@@ -650,35 +672,40 @@
     copies1 = everyone(summed_slots(copies1, one_plane), one_z, zc, [z_peer(r) for r in z_steps])
     copy2 = gather_core(copies2)
     drain(1)
-    mine = part(one_total, core, 16)
-    mine[...] = summed_slots(copies1, one_z)
-    copy1 = send(mine, mine, sibling)
+    one_half[...] = part(base1, core, 16)[...] - learn_rate * summed_slots(copies1, one_z)
+    far = part(one_out, core, 16)
+    copy1 = send(one_half, far, sibling)
+    put_out(one_half, far)
     copy2.wait_recv()
-    sums2 = jnp.concatenate([total[l * 64:l * 64 + 64] for l in range(7)], axis=1)
-    step2[...] = filt2[...] - learn_rate * sums2[:, :864]
-    off2[...] = bias2[...] - learn_rate * column_to_row(sums2[:, 864:865])
-    outs = [put_out(3), put_out(4)]
     copy1.wait_recv()
-    sums1 = one_total[...]
-    step1[...] = filt1[...] - learn_rate * sums1[:, :108]
-    off1[...] = bias1[...] - learn_rate * column_to_row(sums1[:, 108:109])
-    outs += [put_out(1), put_out(2)]
 
     drain(0)
-    feat_out.wait()
     for out in outs:
         out.wait()
 
 
 def hand_on(*refs):
-    ins, outs, spots, in_sems, out_sems = refs[:5], refs[5:10], refs[10:15], refs[15], refs[16]
-    reads = [pltpu.make_async_copy(ins[n], spots[n], in_sems.at[n]) for n in range(5)]
-    writes = [pltpu.make_async_copy(spots[n], outs[n], out_sems.at[n]) for n in range(5)]
-    for copy in reads:
-        copy.start()
-    for n in (3, 0, 1, 2, 4):
-        reads[n].wait()
-        writes[n].start()
+    ins, outs, spots, results, in_sems, out_sems = refs[:3], refs[3:8], refs[8:11], refs[11:15], refs[15], refs[16]
+    reads = [pltpu.make_async_copy(ins[n], spots[n], in_sems.at[n]) for n in range(3)]
+    feat, one, total = spots
+    step1, off1, step2, off2 = results
+    writes = [pltpu.make_async_copy(a, b, out_sems.at[n]) for n, (a, b) in enumerate(zip((feat,) + results, outs))]
+    for n in (2, 1, 0):
+        reads[n].start()
+    reads[2].wait()
+    for l in range(6):
+        step2[:, 128 * l:128 * l + 128] = total[64 * l:64 * l + 64]
+    step2[:, 768:864] = total[384:448, 0:96]
+    writes[3].start()
+    reads[1].wait()
+    step1[...] = one[:, 0:108]
+    writes[1].start()
+    reads[0].wait()
+    writes[0].start()
+    off1[...] = column_to_row(one[:, 108:109])
+    off2[...] = column_to_row(total[384:448, 96:97])
+    writes[2].start()
+    writes[4].start()
     for copy in writes:
         copy.wait()
 
@@ -702,30 +729,34 @@
         jax.ShapeDtypeStruct((64, 864), f32),
         jax.ShapeDtypeStruct((1, 64), f32),
     )
+    sums = (
+        results[0],
+        jax.ShapeDtypeStruct((32, 128), f32),
+        jax.ShapeDtypeStruct((512, 128), f32),
+    )
     out = pl.pallas_call(
         functools.partial(kernel, (GX, GY, GZ, NX)),
-        out_shape=results,
+        out_shape=sums,
         in_specs=[pl.BlockSpec(memory_space=pltpu.HBM)] * len(operands),
-        out_specs=[pl.BlockSpec(memory_space=pltpu.HBM)] * 5,
+        out_specs=[pl.BlockSpec(memory_space=pltpu.HBM)] * 3,
         scratch_shapes=[
             V((32, 128), bf16), V((2, 4, 16, 128), bf16), V((2, 16, 128), bf16), V((4, 16, 128), bf16),
-            V((16, 128), bf16), V((2, 3, 3, 16, 128), bf16), V((64, 2, 16, 128), bf16), V((4, 8, 32, 256), f32),
+            V((16, 128), bf16), V((2, 3, 3, 16, 128), bf16), V((64, 2, 16, 128), bf16), V((8, 128, 256), f32),
             V((2, 128, 64), bf16), V((2, 32, 64), bf16), V((4, 32, 64), bf16),
             V((2, 4, 32, 128), bf16), V((2, 2, 32, 128), bf16), V((2, 2, 4, 32, 128), bf16),
             V((2, 2, 32, 128), bf16), V((4, 2, 32, 128), bf16), V((48, 32, 128), bf16),
             V((16, 128), bf16), V((2, 3, 3, 16, 128), bf16), V((48, 96, 128), bf16),
             V((4, 6, 64, 128), bf16), V((32, 256), bf16), V((2, 32, 256), bf16), V((24, 192, 128), bf16),
-            V((32, 1792), bf16), V((2, 8, 32, 128), f32),
+            V((64, 2304), bf16), V((2, 8, 32, 128), f32),
             V((512, 128), f32), V((256, 128), f32), V((256, 128), f32), V((NP - 1, n3, 128), f32),
             V((NZ, n3, 128), f32),
             V((512, 128), f32),
             V((32, 128), f32), V((16, 128), f32), V((NP, 16, 128), f32),
-            V((NZ, 16, 128), f32), V((32, 128), f32),
+            V((NZ, 16, 128), f32), V((16, 128), f32),
             pltpu.SemaphoreType.DMA((sems,)), pltpu.SemaphoreType.DMA((sems,)),
         ] + [V(a.shape, a.dtype) for a in operands] + [
             pltpu.SemaphoreType.DMA((len(operands),)),
-        ] + [V(a.shape, a.dtype) for a in results] + [
-            pltpu.SemaphoreType.DMA((5,)),
+            V((128, 64), bf16), V((32, 128), f32), V((512, 128), f32), pltpu.SemaphoreType.DMA((3,)),
         ],
         compiler_params=pltpu.CompilerParams(
             collective_id=0, has_side_effects=True, vmem_limit_bytes=62 * 2**20
@@ -734,10 +765,10 @@
     out = pl.pallas_call(
         hand_on,
         out_shape=results,
-        in_specs=[pl.BlockSpec(memory_space=pltpu.HBM)] * 5,
+        in_specs=[pl.BlockSpec(memory_space=pltpu.HBM)] * 3,
         out_specs=[pl.BlockSpec(memory_space=pltpu.HBM)] * 5,
-        scratch_shapes=[V(a.shape, a.dtype) for a in results]
-        + [pltpu.SemaphoreType.DMA((5,)), pltpu.SemaphoreType.DMA((5,))],
+        scratch_shapes=[V(a.shape, a.dtype) for a in sums + results[1:]]
+        + [pltpu.SemaphoreType.DMA((3,)), pltpu.SemaphoreType.DMA((5,))],
         compiler_params=pltpu.CompilerParams(vmem_limit_bytes=62 * 2**20),
     )(*out)
     features, stepped_first, offset_first, stepped_second, offset_second = out

time: 52.4 us -> 51.6 us (0.985)
  Pallas kernels: 51.7 us -> 50.9 us
    pallas_call x1, Pallas kernels: 49.9 us -> 49.2 us  [shards(): pl.pallas_call(functools.partial(kernel, (GX, GY, GZ, NX)), out_shape=sum...]
where the time goes in v8:
time: 51.6 us; the launch traced here: 51.5 us
  Pallas kernels  50.9 us (99%)
  between operations  0.64 us (1%)
    pallas_call x1, Pallas kernels, shards(): pl.pallas_call(functools.partial(kernel, (GX, GY, GZ, NX)), out_shape=sum...  49.2 us
    pallas_call x1, Pallas kernels, shards(): pl.pallas_call(hand_on, out_shape=results, in_specs=[pl.BlockSpec(memory_...  1.74 us

profile of v8, /device:TPU:1, one launch (start us, length us, event | category | flops | bytes accessed | tf_op | source)
XLA Modules:
  0.0 51.5 jit_solution(1715854316059886430)
XLA Ops:
  0.6 49.2 %shard_map.110 = (bf16[128,64]{1,0:T(8,128)(2,1)}, f32[32,128]{1,0:T(8,128)}, f32[512,128]{1,0:T(8,128)}) custom-call(bf16[4,4,16,128]{3,2,1,0:T(8,128)(2,1)} %refs_0_.1, f32[32,108]{1,0:T(8,128)} %refs_1_.1, f32[1,32]{1,0:T(1,128)} %bitcast.11, f32[64,864]{1,0:T(8,128)} %refs_3_.1, f32[1,64]{1,0:T(1,128)} %bitcast.12, bf16[128,64]{1,0:T(8,128)(2,1)} %bitcast.10, ...), custom_call_target="tpu_custom_call" | custom-call | tf_op jit(solution)/shard_map/pallas_call | solution.py:737
  49.8 1.7 %shard_map.111 = (bf16[128,64]{1,0:T(8,128)(2,1)}, f32[32,108]{1,0:T(8,128)}, f32[1,32]{1,0:T(1,128)}, f32[64,864]{1,0:T(8,128)}, f32[1,64]{1,0:T(1,128)}) custom-call(bf16[128,64]{1,0:T(8,128)(2,1)} %get-tuple-element.13.refs_0_, f32[32,128]{1,0:T(8,128)} %get-tuple-element.14.refs_1_, f32[512,128]{1,0:T(8,128)} %get-tuple-element.15.refs_2_), custom_call_target="tpu_custom_call" | custom-call | tf_op jit(solution)/shard_map/pallas_call | solution.py:765

commit v9 on v8

--- a/solution.py
+++ b/solution.py
@@ -220,8 +220,7 @@
     ) = refs[3:]
     near = (vol, filt1, bias1, filt2, bias2, cot, packed)
     fetches = [pltpu.make_async_copy(a, b, in_sems.at[n]) for n, (a, b) in enumerate(zip(far, near))]
-    for fetch in fetches:
-        fetch.start()
+    fetches[0].start()
     t = {name: Rows(packed, name) for name in TABLE}
 
     gx, gy, gz = lax.axis_index("gx"), lax.axis_index("gy"), lax.axis_index("gz")
@@ -296,6 +295,8 @@
     wanted = jnp.where(row < 16, row * 16, row * 16 - 241)
     edge = jnp.where(column == wanted, 1.0, 0.0).astype(bf16)
     fetches[0].wait()
+    for fetch in fetches[1:]:
+        fetch.start()
     block = vol[...].reshape(256, 128)
     edges[...] = mm(edge, block).astype(bf16)
     pl.semaphore_wait(barrier, len(peers))
@@ -476,9 +477,7 @@
             for a in range(2):
                 copies.append(send(packs.at[b], corner2.at[a * 2 + b], shifted(1 - 2 * a, 0, 1 - 2 * b)))
     pick = t["pick2"][...]
-    ends = sum(
-        mm(pick[:, 128 * dq:128 * dq + 128], pooled[:, dq].reshape(64, 128), NT) for dq in range(4)
-    )
+    ends = mm(pick, jnp.concatenate([pooled[:, dq].reshape(64, 128) for dq in range(4)], axis=1), NT)
     col2[...] = jnp.concatenate([ends, jnp.zeros((16, 64), f32)], axis=1).astype(bf16)
     copies_c = send_columns(col2, col2_in)
 
@@ -557,12 +556,9 @@
         ]
         feat[...] = (mm(t["collect"][0:128], ends[0], NT) + mm(t["collect"][128:256], ends[1], NT)).astype(bf16)
         ones_rows = [jnp.ones((32, 128), bf16)]
-        grad2 = None
-        for dq in range(4):
-            cols = jnp.concatenate([cols2(w, dq + 1, ones_rows) for w in (1, 2)], axis=1)
-            err = jnp.concatenate([errs[w, dq + 1] for w in (1, 2)], axis=1)
-            piece = mm(err, cols, NT)
-            grad2 = piece if grad2 is None else grad2 + piece
+        cols = jnp.concatenate([cols2(w, dq, ones_rows) for dq in range(1, 5) for w in (1, 2)], axis=1)
+        err = jnp.concatenate([errs[w, dq] for dq in range(1, 5) for w in (1, 2)], axis=1)
+        grad2 = mm(err, cols, NT)
         for l in range(7):
             grads[l * 64:l * 64 + 64] = grad2[:, 128 * l:128 * l + 128]
         grads[448:512] = jnp.zeros((64, 128), f32)
@@ -618,14 +614,16 @@
             acc = acc + slots[n]
         return acc
 
-    errors(range(0, 6), [(1, 2), (0, 3)])
+    errors(range(1, 5), [(1, 2)])
+    copies2 = second_half_grads()
+    errors((0, 5), [(1, 2), (0, 3)])
+    errors(range(1, 5), [(0, 3)])
     pick = t["pick3"][...]
-    col3[...] = sum(
-        mm(pick[:, 128 * dq:128 * dq + 128], errs[:, dq].reshape(256, 128), NT) for dq in range(6)
-    ).astype(bf16)
+    every = jnp.concatenate([errs[:, dq].reshape(256, 128) for dq in range(6)], axis=1)
+    col3[...] = mm(pick[:, :768], every, NT).astype(bf16)
     copies = [send(col3, col3_in.at[0], shifted(0, 1, 0)), send(col3, col3_in.at[1], shifted(0, -1, 0))]
 
-    copies2 = sum_core(second_half_grads())
+    copies2 = sum_core(copies2)
     inner = mm(errs[...].reshape(1536, 128), t["shift2"][...])
     arrive(copies)
     rows = [kept(has_below, col3_in[0]), kept(has_above, col3_in[1])]
@@ -661,15 +659,16 @@
     grad1 = sum(grad1[32 * w:32 * w + 32, 48 * w:48 * w + 144] for w in range(4))
     one[...] = sum(mm(piece, t["narrow"][...]) for piece in split3(grad1))
     copies1 = send(part(one, 1 - core, 16), one_core, sibling)
-    copies2 = sum_plane(copies2)
-    drain(NP + NZ)
+    drain(NP + 1)
     copies1.wait_recv()
     copies1 = everyone(
         part(one, core, 16)[...] + one_core[...], one_plane, plane, [plane_peer(step)[1] for step in plane_steps]
     )
+    copies2 = sum_plane(copies2)
+    drain(NP + NZ)
+    copies1 = everyone(summed_slots(copies1, one_plane), one_z, zc, [z_peer(r) for r in z_steps])
+    copies2 = sum_z(copies2)
     drain(NP)
-    copies2 = sum_z(copies2)
-    copies1 = everyone(summed_slots(copies1, one_plane), one_z, zc, [z_peer(r) for r in z_steps])
     copy2 = gather_core(copies2)
     drain(1)
     one_half[...] = part(base1, core, 16)[...] - learn_rate * summed_slots(copies1, one_z)

time: 51.6 us -> 51.6 us (level)
  no operation moved by 1% of the time
where the time goes in v9:
time: 51.6 us; the launch traced here: 51.5 us
  Pallas kernels  50.8 us (98%)
  between operations  0.64 us (1%)
    pallas_call x1, Pallas kernels, shards(): pl.pallas_call(functools.partial(kernel, (GX, GY, GZ, NX)), out_shape=sum...  49.1 us
    pallas_call x1, Pallas kernels, shards(): pl.pallas_call(hand_on, out_shape=results, in_specs=[pl.BlockSpec(memory_...  1.74 us

profile of v9, /device:TPU:1, one launch (start us, length us, event | category | flops | bytes accessed | tf_op | source)
XLA Modules:
  0.0 51.5 jit_solution(18064359434314879719)
XLA Ops:
  0.6 49.1 %shard_map.110 = (bf16[128,64]{1,0:T(8,128)(2,1)}, f32[32,128]{1,0:T(8,128)}, f32[512,128]{1,0:T(8,128)}) custom-call(bf16[4,4,16,128]{3,2,1,0:T(8,128)(2,1)} %refs_0_.1, f32[32,108]{1,0:T(8,128)} %refs_1_.1, f32[1,32]{1,0:T(1,128)} %bitcast.11, f32[64,864]{1,0:T(8,128)} %refs_3_.1, f32[1,64]{1,0:T(1,128)} %bitcast.12, bf16[128,64]{1,0:T(8,128)(2,1)} %bitcast.10, ...), custom_call_target="tpu_custom_call" | custom-call | tf_op jit(solution)/shard_map/pallas_call | solution.py:736
  49.7 1.7 %shard_map.111 = (bf16[128,64]{1,0:T(8,128)(2,1)}, f32[32,108]{1,0:T(8,128)}, f32[1,32]{1,0:T(1,128)}, f32[64,864]{1,0:T(8,128)}, f32[1,64]{1,0:T(1,128)}) custom-call(bf16[128,64]{1,0:T(8,128)(2,1)} %get-tuple-element.13.refs_0_, f32[32,128]{1,0:T(8,128)} %get-tuple-element.14.refs_1_, f32[512,128]{1,0:T(8,128)} %get-tuple-element.15.refs_2_), custom_call_target="tpu_custom_call" | custom-call | tf_op jit(solution)/shard_map/pallas_call | solution.py:764

commit v10 on v8

--- a/solution.py
+++ b/solution.py
@@ -600,12 +600,18 @@
         mine[...] = part(base2, core * NP + plane, n3)[...] - learn_rate * acc
         return [send(mine, mine, plane_peer(step)[1]) for step in plane_steps]
 
+    def forward(p):
+        row = core * NP + p
+        return send(part(total, row, n3), part(total_out, row, n3), sibling)
+
     def gather_core(copies):
-        arrive(copies)
-        mine, far = part(total, core, n1), part(total_out, core, n1)
-        copy = send(mine, far, sibling)
-        put_out(mine, far)
-        return copy
+        copies_on = [forward(plane)]
+        for copy, step in reversed(list(zip(copies, plane_steps))):
+            copy.wait_recv()
+            px, py = lax.rem(xc + NX - step[0], NX), lax.rem(gy + GY - step[1], GY)
+            copies_on.append(forward(px * GY + py))
+        put_out(part(total, core, n1), part(total_out, core, n1))
+        return copies_on
 
     def everyone(value, slots, index, devices):
         slots[index] = value
@@ -670,13 +676,13 @@
     drain(NP)
     copies2 = sum_z(copies2)
     copies1 = everyone(summed_slots(copies1, one_plane), one_z, zc, [z_peer(r) for r in z_steps])
-    copy2 = gather_core(copies2)
-    drain(1)
+    copies2 = gather_core(copies2)
+    drain(NP)
     one_half[...] = part(base1, core, 16)[...] - learn_rate * summed_slots(copies1, one_z)
     far = part(one_out, core, 16)
     copy1 = send(one_half, far, sibling)
     put_out(one_half, far)
-    copy2.wait_recv()
+    arrive(copies2)
     copy1.wait_recv()
 
     drain(0)
@@ -720,7 +726,7 @@
         volume, first_filters, first_bias.reshape(1, 32), second_filters, second_bias.reshape(1, 64),
         cotangent.transpose(1, 2, 3, 0).reshape(128, 64), jnp.asarray(PACKED),
     ]
-    sems = 68 + 4 + 3 * (NP - 1) + 2 * (NZ - 1)
+    sems = 68 + 4 + 4 * (NP - 1) + 2 * (NZ - 1)
     V = pltpu.VMEM
     results = (
         jax.ShapeDtypeStruct((128, 64), bf16),

time: 51.6 us -> 51.9 us (level)
  no operation moved by 1% of the time
where the time goes in v10:
time: 51.9 us; the launch traced here: 51.8 us
  Pallas kernels  51.2 us (99%)
  between operations  0.64 us (1%)
    pallas_call x1, Pallas kernels, shards(): pl.pallas_call(functools.partial(kernel, (GX, GY, GZ, NX)), out_shape=sum...  49.4 us
    pallas_call x1, Pallas kernels, shards(): pl.pallas_call(hand_on, out_shape=results, in_specs=[pl.BlockSpec(memory_...  1.74 us

profile of v10, /device:TPU:1, one launch (start us, length us, event | category | flops | bytes accessed | tf_op | source)
XLA Modules:
  0.0 51.8 jit_solution(10504253653772020866)
XLA Ops:
  0.6 49.4 %shard_map.110 = (bf16[128,64]{1,0:T(8,128)(2,1)}, f32[32,128]{1,0:T(8,128)}, f32[512,128]{1,0:T(8,128)}) custom-call(bf16[4,4,16,128]{3,2,1,0:T(8,128)(2,1)} %refs_0_.1, f32[32,108]{1,0:T(8,128)} %refs_1_.1, f32[1,32]{1,0:T(1,128)} %bitcast.11, f32[64,864]{1,0:T(8,128)} %refs_3_.1, f32[1,64]{1,0:T(1,128)} %bitcast.12, bf16[128,64]{1,0:T(8,128)(2,1)} %bitcast.10, ...), custom_call_target="tpu_custom_call" | custom-call | tf_op jit(solution)/shard_map/pallas_call | solution.py:743
  50.1 1.7 %shard_map.111 = (bf16[128,64]{1,0:T(8,128)(2,1)}, f32[32,108]{1,0:T(8,128)}, f32[1,32]{1,0:T(1,128)}, f32[64,864]{1,0:T(8,128)}, f32[1,64]{1,0:T(1,128)}) custom-call(bf16[128,64]{1,0:T(8,128)(2,1)} %get-tuple-element.13.refs_0_, f32[32,128]{1,0:T(8,128)} %get-tuple-element.14.refs_1_, f32[512,128]{1,0:T(8,128)} %get-tuple-element.15.refs_2_), custom_call_target="tpu_custom_call" | custom-call | tf_op jit(solution)/shard_map/pallas_call | solution.py:771
